TPU v7x, 256 devices: a whole 4x4x8 slice. The times are simulated.
256 devices in a mesh: state: 16 (over y, z_lo), tile: 16 (over z_hi, x, core).
Axes of the slice: x: 4, y: 4, z: 8 (z_hi: 2, z_lo: 4; z = z_hi * 4 + z_lo), core: 2. Of those that a mesh axis runs over, the one named last changes fastest.
Arguments:
- pair_tiles: bfloat16 [16, 16, 32, 32, 128], P('state', 'tile'), may hold values from -60 to 60
- targets: int32 [16, 16, 2, 4, 128], P('state', 'tile'), may hold values from 0 to 63, as said below
- offsets: int32 [16], replicated, may hold values from 0 to 128, as said below
- ln_gain: float32 [128], replicated, may hold values from 0.5 to 1.5
- ln_bias: float32 [128], replicated, may hold values from -3 to 3
- w_query: bfloat16 [128, 128], replicated, may hold values from -0.5 to 0.5
- w_key: bfloat16 [128, 128], replicated, may hold values from -0.5 to 0.5
- w_value: bfloat16 [128, 128], replicated, may hold values from -0.5 to 0.5
- w_pairbias: float32 [128, 4], replicated, may hold values from -25 to 25
- w_gate: bfloat16 [128, 128], replicated, may hold values from -0.5 to 0.5
- gate_bias: float32 [128], replicated, may hold values from -4 to 4
- w_output: bfloat16 [128, 128], replicated, may hold values from -0.5 to 0.5
- out_bias: float32 [128], replicated, may hold values from -3 to 3
- w_distogram: float32 [128, 64], replicated, may hold values from -4 to 4
- dist_bias: float32 [64], replicated, may hold values from -4 to 4
Outputs:
- shared_grad: float32 [8, 16, 2, 2, 128, 128], P(None, 'tile', None, None, 'state')
Inputs may be any that keep to these rules, and one draw needn't show every extreme that they name: `targets`: symmetric: the bin of crop pair (x, y) equals that of (y, x) in every state. `offsets`: each is a multiple of 32; some state starts at 0 and some state at 128.
All inputs are finite; a program needn't handle non-finite values.
Results may differ from a plain program's by a relative error of at most 0.015.
Values may be sent and summed in bfloat16 or wider, within the bound.
A program may use at most 64 MiB of HBM per device.

v0:
```python
import math

import jax
import jax.numpy as jnp
from jax import lax
from jax.sharding import PartitionSpec as P

C = 128
H = 4
HD = 32
NB = 64
L = 128


def layer_norm(pair_field, ln_gain, ln_bias):
    center = pair_field - jnp.mean(pair_field, axis=-1, keepdims=True)
    inverse = lax.rsqrt(jnp.mean(center * center, axis=-1, keepdims=True) + 1e-05)
    normed = center * inverse
    return (normed * ln_gain + ln_bias, normed, inverse)


def probabilities(queries, key_proj, bias_full):
    scores = jnp.einsum("rjhd,rkhd->rhjk", queries, key_proj, preferred_element_type=jnp.float32)
    scores = scores * (1.0 / math.sqrt(HD)) + bias_full[None]
    row_max = jnp.max(scores, axis=-1, keepdims=True)
    exp_scores = jnp.exp(scores - row_max)
    return exp_scores / jnp.sum(exp_scores, axis=-1, keepdims=True)


def on_device(
    pair_tiles,
    targets,
    offsets,
    ln_gain,
    ln_bias,
    w_query,
    w_key,
    w_value,
    w_pairbias,
    w_gate,
    gate_bias,
    w_output,
    out_bias,
    w_distogram,
    dist_bias,
):
    tile_count = lax.axis_size("tile")
    state_count = lax.axis_size("state")
    tile_side = pair_tiles.shape[2]
    tile_grid = L // tile_side
    row_share = tile_side // tile_count
    rows_here = row_share * tile_grid
    hidden_width = H * HD
    inv_root = 1.0 / math.sqrt(HD)
    block_rows = 2
    groups = rows_here // block_rows

    def split_rows(values_in):
        return values_in.reshape((groups, block_rows) + values_in.shape[1:])

    blocked = pair_tiles[0, 0].reshape(tile_count, row_share, tile_side, C)
    regrouped = lax.all_to_all(blocked, "tile", split_axis=0, concat_axis=2, tiled=True)
    pair_field = regrouped.reshape(rows_here, L, C).astype(jnp.float32)
    normed_out, normed, inverse = layer_norm(pair_field, ln_gain, ln_bias)
    flat_b = normed_out.astype(jnp.bfloat16).reshape(rows_here * L, C)

    def project(weight):
        return (
            jnp.dot(flat_b, weight, preferred_element_type=jnp.float32)
            .astype(jnp.bfloat16)
            .reshape(rows_here, L, H, HD)
        )

    queries = project(w_query)
    key_proj = project(w_key)
    value_proj = project(w_value)
    gate_act = jax.nn.sigmoid(
        jnp.dot(flat_b, w_gate, preferred_element_type=jnp.float32) + gate_bias
    ).reshape(rows_here, L, hidden_width)
    bias_rows = jnp.einsum("rlc,ch->hrl", normed_out, w_pairbias, precision=lax.Precision.HIGHEST)
    gathered = lax.all_gather(bias_rows, "tile", axis=1, tiled=True)
    bias_full = (
        gathered.reshape(H, tile_count, row_share, tile_grid, L)
        .transpose(0, 3, 1, 2, 4)
        .reshape(H, L, L)
    )

    def forward_block(block_args):
        query_blk, key_blk, value_blk = block_args
        weights_b = probabilities(query_blk, key_blk, bias_full).astype(jnp.bfloat16)
        return jnp.einsum(
            "rhjk,rkhd->rjhd", weights_b, value_blk, preferred_element_type=jnp.float32
        )

    attended = lax.map(
        forward_block, (split_rows(queries), split_rows(key_proj), split_rows(value_proj))
    ).reshape(rows_here, L, hidden_width)
    gated_out = (gate_act * attended).astype(jnp.bfloat16)
    updated = (
        pair_field
        + jnp.dot(
            gated_out.reshape(rows_here * L, hidden_width),
            w_output,
            preferred_element_type=jnp.float32,
        ).reshape(rows_here, L, C)
        + out_bias
    )
    outgoing = updated.reshape(row_share, tile_grid, tile_grid, tile_count, row_share * C)
    incoming = lax.all_to_all(
        outgoing.astype(jnp.bfloat16), "tile", split_axis=3, concat_axis=3, tiled=True
    ).astype(outgoing.dtype)
    mirrored = (
        incoming.reshape(row_share, tile_grid, tile_grid, tile_count, row_share, C)
        .transpose(4, 2, 1, 3, 0, 5)
        .reshape(rows_here, L, C)
    )
    logits = (
        jnp.einsum("rlc,cb->rlb", updated + mirrored, w_distogram, precision=lax.Precision.HIGHEST)
        + dist_bias
    )
    row_max = jnp.max(logits, axis=-1, keepdims=True)
    exp_logits = jnp.exp(logits - row_max)
    bin_prob = exp_logits / jnp.sum(exp_logits, axis=-1, keepdims=True)
    target_here = targets.reshape(rows_here, L)
    onehot = (target_here[:, :, None] == jnp.arange(NB, dtype=jnp.int32)[None, None, :]).astype(
        jnp.float32
    )
    logit_grad = 2.0 * (bin_prob - onehot)
    pair_grad = jnp.einsum("rlb,cb->rlc", logit_grad, w_distogram, precision=lax.Precision.HIGHEST)
    out_grad = jnp.einsum(
        "rlc,wc->rlw", pair_grad.astype(jnp.bfloat16), w_output, preferred_element_type=jnp.float32
    )
    att_grad_b = (out_grad * gate_act).astype(jnp.bfloat16).reshape(rows_here, L, H, HD)
    gate_grad = out_grad * attended * gate_act * (1.0 - gate_act)

    def backward_block(bias_sum, block_args):
        query_blk, key_blk, value_blk, grad_blk = block_args
        attn_prob = probabilities(query_blk, key_blk, bias_full)
        weights_b = attn_prob.astype(jnp.bfloat16)
        value_grad = jnp.einsum(
            "rhjk,rjhd->rkhd", weights_b, grad_blk, preferred_element_type=jnp.float32
        )
        weight_grad = jnp.einsum(
            "rjhd,rkhd->rhjk", grad_blk, value_blk, preferred_element_type=jnp.float32
        )
        score_grad = attn_prob * (
            weight_grad - jnp.sum(attn_prob * weight_grad, axis=-1, keepdims=True)
        )
        score_b = score_grad.astype(jnp.bfloat16)
        query_grad = (
            jnp.einsum("rhjk,rkhd->rjhd", score_b, key_blk, preferred_element_type=jnp.float32)
            * inv_root
        )
        key_grad = (
            jnp.einsum("rhjk,rjhd->rkhd", score_b, query_blk, preferred_element_type=jnp.float32)
            * inv_root
        )
        return (bias_sum + jnp.sum(score_grad, axis=0), (query_grad, key_grad, value_grad))

    bias_grad, grad_parts = lax.scan(
        backward_block,
        jnp.zeros((H, L, L), jnp.float32),
        (split_rows(queries), split_rows(key_proj), split_rows(value_proj), split_rows(att_grad_b)),
    )
    query_grad, key_grad, value_grad = grad_parts
    owner_order = (
        bias_grad.reshape(H, tile_grid, tile_count, row_share, L)
        .transpose(0, 2, 3, 1, 4)
        .reshape(H, L, L)
    )
    bias_share = lax.psum_scatter(
        owner_order.astype(jnp.bfloat16), "tile", scatter_dimension=1, tiled=True
    ).astype(jnp.float32)

    def back_project(grad_part, weight):
        return jnp.einsum(
            "rlw,cw->rlc",
            grad_part.reshape(rows_here, L, hidden_width).astype(jnp.bfloat16),
            weight,
            preferred_element_type=jnp.float32,
        )

    normed_grad = (
        back_project(query_grad, w_query)
        + back_project(key_grad, w_key)
        + back_project(value_grad, w_value)
        + back_project(gate_grad, w_gate)
    )
    normed_grad = normed_grad + jnp.einsum(
        "hrl,ch->rlc", bias_share, w_pairbias, precision=lax.Precision.HIGHEST
    )
    scaled = normed_grad * ln_gain
    ln_back = inverse * (
        scaled
        - jnp.mean(scaled, axis=-1, keepdims=True)
        - normed * jnp.mean(scaled * normed, axis=-1, keepdims=True)
    )
    total_grad = (pair_grad + ln_back).astype(jnp.bfloat16)
    state_here = lax.axis_index("state")
    piece_cols = L // state_count
    shifted = jnp.roll(total_grad, offsets[state_here], axis=1)
    outgoing_rows = shifted.reshape(rows_here, state_count, piece_cols, C)
    received = lax.all_to_all(outgoing_rows, "state", split_axis=1, concat_axis=1, tiled=True)
    placed = (
        received.astype(jnp.float32)
        .reshape(row_share, tile_grid, state_count, piece_cols, C)
        .transpose(2, 1, 0, 3, 4)
    )
    columns = state_here * piece_cols + jnp.arange(piece_cols, dtype=jnp.int32)
    full_blocks = 2 * tile_grid

    def place(source, accum):
        offset = offsets[source]
        high_half = (columns < offset).astype(jnp.float32)[:, None]
        incoming_blk = lax.dynamic_index_in_dim(placed, source, 0, keepdims=False)
        contrib = jnp.stack([incoming_blk * (1.0 - high_half), incoming_blk * high_half], axis=2)
        row_start = offset // tile_side
        zero_index = jnp.zeros((), jnp.int32)
        corner = (row_start, zero_index, zero_index, zero_index, zero_index)
        window = lax.dynamic_slice(accum, corner, contrib.shape)
        return lax.dynamic_update_slice(accum, window + contrib, corner)

    accum = lax.fori_loop(
        0, state_count, place, jnp.zeros((full_blocks, row_share, 2, piece_cols, C), jnp.float32)
    )
    return accum.reshape(full_blocks, 1, row_share, 2, piece_cols, C)


def solution(mesh):
    in_specs = (
        P("state", "tile", None, None, None),
        P("state", "tile", None, None, None),
        P(),
        P(),
        P(),
        P(),
        P(),
        P(),
        P(),
        P(),
        P(),
        P(),
        P(),
        P(),
        P(),
    )
    out_specs = P(None, "tile", None, None, "state", None)
    return jax.shard_map(
        on_device, mesh=mesh, in_specs=in_specs, out_specs=out_specs, check_vma=False
    )
```

profile of v0, /device:TPU:1, one launch (start us, length us, event | category | flops | bytes accessed | tf_op | source)
XLA Modules:
  0.0 375.3 jit_solution(2915927126288467536)
XLA Ops:
  6.5 12.6 %all-to-all-start = ((bf16[16,2,32,128]{3,2,1,0:T(8,128)(2,1)}), bf16[16,2,32,128]{3,2,1,0:T(8,128)(2,1)S(1)}, u32[]{:S(2)}, u32[]{:S(2)}) async-start(bf16[16,2,32,128]{3,2,1,0:T(8,128)(2,1)} %bitcast.301), calls=%async_computation | async-start | bytes 524288 | tf_op jit(solution)/shard_map/all_to_all | solution.py:62
  19.1 11.1 %all-to-all-done = bf16[16,2,32,128]{3,2,1,0:T(8,128)(2,1)S(1)} async-done(((bf16[16,2,32,128]{3,2,1,0:T(8,128)(2,1)}), bf16[16,2,32,128]{3,2,1,0:T(8,128)(2,1)S(1)}, u32[]{:S(2)}, u32[]{:S(2)}) %all-to-all-start) | async-done | bytes 262176 | tf_op jit(solution)/shard_map/all_to_all | solution.py:62
  31.8 0.8 convolution_bitcast_fusion.2
  32.6 26.3 %all_gather.3 = f32[4,128,128]{2,0,1:T(4,128)S(1)} all-gather(f32[4,8,128]{2,0,1:T(4,128)S(1)} %convolution_bitcast_fusion.2), channel_id=1, replica_groups=mesh['state'=16,'tile'=16] {'tile'}, dimensions={1}, use_global_device_ids=true | all-gather | bytes 278528 | tf_op jit(solution)/shard_map/all_gather | solution.py:81
  60.5 0.7 copy-done.12
  61.7 0.7 copy-done.14
  63.0 4.3 %while.46 = (s32[]{:T(128)}, f32[4,2,128,4,32]{2,4,3,1,0:T(8,128)S(1)}, bf16[4,2,128,4,32]{2,4,3,1,0:T(8,128)(2,1)S(1)}, bf16[4,2,128,4,32]{2,4,3,1,0:T(8,128)(2...) while((s32[]{:T(128)}, ...), condition=%wide.region_5.6_spmd.clone, body=%wide.region_2.5_spmd.sunk.clone | while | flops 26346752 | bytes 3091533 | solution.py:95
  67.3 0.7 copy-done.11
  70.3 0.6 copy-done.23
  71.3 0.8 copy.209
  72.1 7.1 %all-to-all-start.1 = ((bf16[2,4,4,16,256]{4,2,1,0,3:T(4,128)(2,1)}), bf16[2,4,4,16,256]{4,2,1,0,3:T(4,128)(2,1)}, u32[]{:S(2)}, u32[]{:S(2)}) async-start(bf16[2,4,4,16,256]{4,2,1,0,3:T(4,128)(2,1)} %copy.209), calls=%async_computation.1 | async-start | bytes 524288 | tf_op jit(solution)/shard_map/all_to_all | solution.py:109
  79.5 0.6 copy-done.26
  82.7 0.7 copy.283
  83.4 0.7 copy.282
  84.1 0.7 copy-done.28
  86.2 4.3 %all-to-all-done.1 = bf16[2,4,4,16,256]{4,2,1,0,3:T(4,128)(2,1)} async-done(((bf16[2,4,4,16,256]{4,2,1,0,3:T(4,128)(2,1)}), bf16[2,4,4,16,256]{4,2,1,0,3:T(4,128)(2,1)}, u32[]{:S(2)}, u32[]{:S(2)}) %all-to-all-start.1) | async-done | bytes 262176 | tf_op jit(solution)/shard_map/all_to_all | solution.py:109
  90.5 1.1 copy_convert_fusion
  91.6 1.1 reshape.191
  92.6 1.5 copy.211
  94.1 0.6 copy-done.22
  94.7 0.7 convolution_add_fusion.6
  95.8 0.7 copy-done.24
  96.5 1.0 fusion.102
  97.5 1.1 multiply_convert_fusion.1
  98.6 20.4 %while.48 = (s32[]{:T(128)}, f32[4,128,128]{1,2,0:T(8,128)S(1)}, bf16[4,2,128,4,32]{2,4,3,1,0:T(8,128)(2,1)S(1)}, bf16[4,2,128,4,32]{2,4,3,1,0:T(8,128)(2,1)}, b...) while((s32[]{:T(128)}, f32[4,128,128]{1,2,0:T(8,128)S(1)}, ...), condition=%wide.region_13.14_spmd.clone.clone, body=%wide.region_8.13_spmd.clone.sunk.clone | while | flops 52691200 | bytes 8616111 | solution.py:160
  99.2 1.3 fusion.236
  100.5 1.2 multiply_reduce_fusion.4
  101.9 0.9 copy-done.8
  104.3 1.3 fusion.236
  105.6 1.2 multiply_reduce_fusion.4
  107.0 0.9 copy-done.8
  109.4 1.3 fusion.236
  110.7 1.2 multiply_reduce_fusion.4
  112.1 0.9 copy-done.8
  114.5 1.3 fusion.236
  115.8 1.2 multiply_reduce_fusion.4
  117.2 0.9 copy-done.8
  119.2 0.8 copy.228
  120.3 0.7 copy-done.10
  121.5 0.7 copy-done.3
  122.7 172.3 %all-reduce.3.cloned.1.call-done = bf16[4,128,128]{2,0,1:T(4,128)(2,1)} async-done(((bf16[4,128,128]{2,0,1:T(4,128)(2,1)}), bf16[4,128,128]{2,0,1:T(4,128)(2,1)}) %all-reduce.3.cloned.1.call-update) | async-done | bytes 131088
  295.0 1.7 fusion.129
  297.5 0.8 copy.230
  298.3 4.4 %all-to-all-start.2 = ((bf16[8,16,8,128]{3,2,0,1:T(8,128)(2,1)}), bf16[8,16,8,128]{3,2,0,1:T(8,128)(2,1)S(1)}, u32[]{:S(2)}, u32[]{:S(2)}) async-start(bf16[8,16,8,128]{3,2,0,1:T(8,128)(2,1)} %copy.230), calls=%async_computation.2 | async-start | bytes 524288 | tf_op jit(solution)/shard_map/all_to_all | solution.py:203
  302.7 8.1 %all-to-all-done.2 = bf16[8,16,8,128]{3,2,0,1:T(8,128)(2,1)S(1)} async-done(((bf16[8,16,8,128]{3,2,0,1:T(8,128)(2,1)}), bf16[8,16,8,128]{3,2,0,1:T(8,128)(2,1)S(1)}, u32[]{:S(2)}, u32[]{:S(2)}) %all-to-all-start.2) | async-done | bytes 262176 | tf_op jit(solution)/shard_map/all_to_all | solution.py:203
  310.9 0.6 copy-done.27
  311.5 56.3 %while.47 = (s32[]{:T(128)}, f32[8,2,2,8,128]{4,3,2,1,0:T(8,128)S(1)}, s32[16]{0:T(128)S(1)}, f32[16,4,2,8,128]{4,3,0,1,2:T(8,128)S(1)}, s32[]{:T(128)}) while((s32[]{:T(128)}, f32[8,2,2,8,128]{4,3,2,1,0:T(8,128)S(1)}, s32[16]{0:T(128)S(1)}, f32[16,4,2,8,128]{4,3,0,1,2:T(8,128)S(1)}, s32[]{:T(128)}) %tuple.142), condition=%wide.region_18.19_spmd.clone.clone, body=%wide.region_17.18_spmd.clone.sunk.clone | while | flops 49204 | bytes 296281 | solution.py:223
  367.9 0.6 copy-done.6
  (208 shorter events, 41.6 us)
Async XLA Ops:
  6.5 63.7 %copy-start = (bf16[128,128]{1,0:T(8,128)(2,1)S(1)}, bf16[128,128]{1,0:T(8,128)(2,1)}, u32[]{:S(2)}) copy-start(bf16[128,128]{1,0:T(8,128)(2,1)} %param.32) | copy-start | bytes 98308
  6.5 23.7 %all-to-all-start = ((bf16[16,2,32,128]{3,2,1,0:T(8,128)(2,1)}), bf16[16,2,32,128]{3,2,1,0:T(8,128)(2,1)S(1)}, u32[]{:S(2)}, u32[]{:S(2)}) async-start(bf16[16,2,32,128]{3,2,1,0:T(8,128)(2,1)} %bitcast.301), calls=%async_computation | async-start | bytes 524288 | tf_op jit(solution)/shard_map/all_to_all | solution.py:62
  31.1 0.7 copy-start.18
  31.2 0.7 copy-start.19
  31.2 0.7 copy-start.21
  59.1 0.8 copy-start.13
  60.4 0.8 copy-start.12
  61.7 0.8 copy-start.14
  67.3 0.7 copy-start.11
  68.0 0.8 copy-start.4
  69.2 0.8 copy-start.16
  69.2 0.8 copy-start.25
  70.3 0.7 copy-start.23
  72.1 18.4 %all-to-all-start.1 = ((bf16[2,4,4,16,256]{4,2,1,0,3:T(4,128)(2,1)}), bf16[2,4,4,16,256]{4,2,1,0,3:T(4,128)(2,1)}, u32[]{:S(2)}, u32[]{:S(2)}) async-start(bf16[2,4,4,16,256]{4,2,1,0,3:T(4,128)(2,1)} %copy.209), calls=%async_computation.1 | async-start | bytes 524288 | tf_op jit(solution)/shard_map/all_to_all | solution.py:109
  79.2 215.8 %all-reduce.3.cloned.1.call-start = ((), (), s32[]{:S(2)}) async-start(), calls=%async_computation.3 | async-start | bytes 262144
  79.4 0.7 copy-start.26
  84.1 0.7 copy-start.28
  92.6 1.5 copy-start.15
  94.1 0.7 copy-start.22
  95.8 0.7 copy-start.24
  97.5 1.1 copy-start.1
  97.5 1.1 copy-start.7
  101.8 1.0 copy-start.8
  103.0 0.7 copy-start.9
  106.9 1.0 copy-start.8
  108.1 0.7 copy-start.9
  112.0 1.0 copy-start.8
  113.2 0.7 copy-start.9
  117.1 1.0 copy-start.8
  118.3 0.7 copy-start.9
  120.0 1.0 copy-start.10
  121.2 1.0 copy-start.3
  121.2 1.2 copy-start.5
  121.2 1.2 copy-start.17
  122.4 172.5 %copy-start.20 = (f32[128]{0:T(128)S(1)}, f32[128]{0:T(128)}, u32[]{:S(2)}) copy-start(f32[128]{0:T(128)} %param.24) | copy-start | bytes 1540
  122.7 174.0 %copy-start.2 = (f32[8,128,128]{2,1,0:T(8,128)S(1)}, f32[8,128,128]{2,1,0:T(8,128)}, u32[]{:S(2)}) copy-start(f32[8,128,128]{2,1,0:T(8,128)} %copy-done.1) | copy-start | bytes 1572868
  298.3 12.5 %all-to-all-start.2 = ((bf16[8,16,8,128]{3,2,0,1:T(8,128)(2,1)}), bf16[8,16,8,128]{3,2,0,1:T(8,128)(2,1)S(1)}, u32[]{:S(2)}, u32[]{:S(2)}) async-start(bf16[8,16,8,128]{3,2,0,1:T(8,128)(2,1)} %copy.230), calls=%async_computation.2 | async-start | bytes 524288 | tf_op jit(solution)/shard_map/all_to_all | solution.py:203
  310.8 0.7 copy-start.27
  367.8 0.7 copy-start.6
Sparse Core Ops, SparseCore 0:
  120.1 174.7 all-reduce.2
where the time goes:
time: 379 us; the launch traced here: 375 us
  waiting for transfers between devices  196 us (52%)
  loops' own time  36.9 us (10%)
  local copies, waits for them, and re-layouts  36.5 us (10%)
  blocking collectives  26.3 us (7%)
  matrix products  24.5 us (6%)
  starting transfers between devices  24.3 us (6%)
  between operations  16.5 us (4%)
  other arithmetic  14.6 us (4%)
    unnamed x2, waiting for transfers between devices  172 us
    another operation x1, loops' own time, on_device(): lax.fori_loop(0, state_count, place, jnp.zeros((full_blocks, row_share, 2...  36.6 us
    all_gather x1, blocking collectives, on_device(): gathered = lax.all_gather(bias_rows, 'tile', axis=1, tiled=True)  26.3 us
    all_to_all x1, starting transfers between devices, on_device(): lax.all_to_all(blocked, 'tile', split_axis=0, concat_axis=2, tiled=True)  12.6 us
    unnamed x57, local copies, waits for them, and re-layouts  12.3 us
    all_to_all x1, waiting for transfers between devices, on_device(): lax.all_to_all(blocked, 'tile', split_axis=0, concat_axis=2, tiled=True)  11.1 us
    dynamic_slice x16, local copies, waits for them, and re-layouts, place(): offset = offsets[source]  9.27 us
    sub x16, other arithmetic, place(): 1.0 - high_half  9.01 us
  transfers between devices with their start and end apart: 4, of which 4 were waited for; matrix products, arithmetic and copies ran while one was open for 1% of the time, Pallas kernels for 0%

commit v1 on v0

v1 whole, which is shorter than its diff:
```python
import math

import jax
import jax.numpy as jnp
from jax import lax
from jax.experimental import pallas as pl
from jax.experimental.pallas import tpu as pltpu
from jax.sharding import PartitionSpec as P

C = 128
H = 4
HD = 32
NB = 64
L = 128
S = 16
T = 16
R = 8
F32 = jnp.float32
BF16 = jnp.bfloat16
I32 = jnp.int32
MESH = pl.DeviceIdType.MESH
LOG2E = 1.0 / math.log(2.0)
INV_ROOT = 1.0 / math.sqrt(HD)

SCRATCH = dict(
    gain_v=pltpu.VMEM((1, C), F32),
    lbias_v=pltpu.VMEM((1, C), F32),
    wq_v=pltpu.VMEM((C, C), BF16),
    wk_v=pltpu.VMEM((C, C), BF16),
    wv_v=pltpu.VMEM((C, C), BF16),
    wg_v=pltpu.VMEM((C, C), BF16),
    wo_v=pltpu.VMEM((C, C), BF16),
    wpb_v=pltpu.VMEM((C, H), F32),
    gbias_v=pltpu.VMEM((1, C), F32),
    obias_v=pltpu.VMEM((1, C), F32),
    wd_v=pltpu.VMEM((C, NB), F32),
    dbias_v=pltpu.VMEM((1, NB), F32),
    targets_v=pltpu.VMEM((2, 4, L), I32),
    w_sem=pltpu.SemaphoreType.DMA((13,)),
    eye=pltpu.VMEM((C, C), BF16),
    hmask=pltpu.VMEM((H, C, C), BF16),
    shift=pltpu.VMEM((L, L), BF16),
    spread=pltpu.VMEM((256, S * 64), BF16),
    w_in_t=pltpu.VMEM((4 * C, C), BF16),
    w_in=pltpu.VMEM((C, 4 * C), BF16),
    wo_t=pltpu.VMEM((C, C), BF16),
    wd_t3=pltpu.VMEM((NB, 3 * C), BF16),
    wd3=pltpu.VMEM((C, 3 * NB), BF16),
    gain_b=pltpu.VMEM((C, L), F32),
    lbias_b=pltpu.VMEM((C, L), F32),
    gbias_b=pltpu.VMEM((C, L), F32),
    obias_b=pltpu.VMEM((C, L), F32),
    dbias_b=pltpu.VMEM((NB, L), F32),
    wpb_b=pltpu.VMEM((H, C, L), F32),
    zb=pltpu.VMEM((R, L, C), BF16),
    zt=pltpu.VMEM((R, C, L), F32),
    xh=pltpu.VMEM((R, C, L), F32),
    inv=pltpu.VMEM((R, 1, L), F32),
    znb=pltpu.VMEM((R, C, L), BF16),
    qt=pltpu.VMEM((R, C, L), BF16),
    kt=pltpu.VMEM((R, C, L), BF16),
    vt=pltpu.VMEM((R, C, L), BF16),
    vn=pltpu.VMEM((R, L, C), BF16),
    gt=pltpu.VMEM((R, C, L), F32),
    ot=pltpu.VMEM((R, C, L), F32),
    at=pltpu.VMEM((R, H, L, L), F32),
    bias_t=pltpu.VMEM((H, L, L), F32),
    lgt=pltpu.VMEM((R, NB, L), F32),
    lgn=pltpu.VMEM((R * L, C), F32),
    mirror=pltpu.VMEM((R, NB, L), F32),
    dp=pltpu.VMEM((R, C, L), F32),
    d4=pltpu.VMEM((R, 4 * C, L), BF16),
    dbt=pltpu.VMEM((H, L, L), F32),
    dbs=pltpu.VMEM((H * R, L), F32),
    grad=pltpu.VMEM((R, L, C), F32),
    tg_stage=pltpu.VMEM((4, 8, L), I32),
    tg_recv=pltpu.VMEM((4, 8, L), I32),
    b_stage=pltpu.VMEM((H * R, L), F32),
    b_recv=pltpu.VMEM((T, H * R, L), F32),
    c_stage=pltpu.VMEM((T, 32, L), BF16),
    c_recv=pltpu.VMEM((T, 32, L), BF16),
    e_stage=pltpu.VMEM((T, 32, L), BF16),
    e_recv=pltpu.VMEM((T, 32, L), BF16),
    f_stage=pltpu.VMEM((4, S, 16, C), BF16),
    f_recv=pltpu.VMEM((S, 4, 16, C), BF16),
    a_send=pltpu.SemaphoreType.DMA((4,)),
    a_sem=pltpu.SemaphoreType.DMA,
    tg_send=pltpu.SemaphoreType.DMA((4,)),
    tg_sem=pltpu.SemaphoreType.DMA,
    b_send=pltpu.SemaphoreType.DMA((16,)),
    b_sem=pltpu.SemaphoreType.DMA((3,)),
    c_send=pltpu.SemaphoreType.DMA((T,)),
    c_sem=pltpu.SemaphoreType.DMA,
    e_send=pltpu.SemaphoreType.DMA((T,)),
    e_sem=pltpu.SemaphoreType.DMA,
    f_send=pltpu.SemaphoreType.DMA((4, S)),
    f_sem=pltpu.SemaphoreType.DMA,
)
NAMES = tuple(SCRATCH)


class Refs:
    pass


def dot(left, right):
    return jnp.dot(left, right, preferred_element_type=F32)


def dot_nt(left, right):
    return lax.dot_general(left, right, (((1,), (1,)), ((), ())), preferred_element_type=F32)


def halves(values):
    high = values.astype(BF16)
    low = (values - high.astype(F32)).astype(BF16)
    return high, low


def three(values):
    high, low = halves(values)
    return jnp.concatenate([high, low, high], axis=0)


def total(values):
    return jnp.sum(values, axis=0, keepdims=True)


def column(row):
    width = row.shape[1]
    return jnp.transpose(jnp.broadcast_to(row, (L, width)))


def kernel(
    tiles,
    targets,
    offsets,
    gain,
    lbias,
    wq,
    wk,
    wv,
    wpb,
    wg,
    gbias,
    wo,
    obias,
    wd,
    dbias,
    out,
    *scratch,
):
    m = Refs()
    for name, ref in zip(NAMES, scratch):
        setattr(m, name, ref)
    state = lax.axis_index("state")
    tile = lax.axis_index("tile")
    band = tile // 4
    sub = tile % 4

    barrier = pltpu.get_barrier_semaphore()

    def greet_tile(step, carry):
        peer = lax.rem(tile + step, T)
        pl.semaphore_signal(barrier, inc=1, device_id=(state, peer), device_id_type=MESH)
        return carry

    lax.fori_loop(1, T, greet_tile, 0)

    def greet_state(step, carry):
        peer = lax.rem(state + step, S)
        for group in range(4):
            pl.semaphore_signal(
                barrier, inc=1, device_id=(peer, 4 * group + band), device_id_type=MESH
            )
        return carry

    lax.fori_loop(1, S, greet_state, 0)

    loads = []
    for index, (source, target) in enumerate(
        [
            (gain, m.gain_v),
            (lbias, m.lbias_v),
            (wq, m.wq_v),
            (wk, m.wk_v),
            (wv, m.wv_v),
            (wg, m.wg_v),
            (wo, m.wo_v),
            (wpb, m.wpb_v),
            (gbias, m.gbias_v),
            (obias, m.obias_v),
            (wd, m.wd_v),
            (dbias, m.dbias_v),
            (targets.at[0, 0], m.targets_v),
        ]
    ):
        load = pltpu.make_async_copy(source, target, m.w_sem.at[index])
        load.start()
        loads.append(load)

    rows_i = lax.broadcasted_iota(I32, (C, C), 0)
    cols_i = lax.broadcasted_iota(I32, (C, C), 1)
    m.eye[...] = jnp.where(rows_i == cols_i, 1.0, 0.0).astype(BF16)
    for head in range(H):
        m.hmask[head] = jnp.where(cols_i // HD == head, 1.0, 0.0).astype(BF16)
    m.shift[...] = jnp.where(((rows_i - offsets[state] + L) & (L - 1)) == cols_i, 1.0, 0.0).astype(BF16)
    rows_o = lax.broadcasted_iota(I32, (256, L), 0)
    cols_o = lax.broadcasted_iota(I32, (256, L), 1)
    row_in = 8 * ((rows_o >> 4) & 1) + (rows_o & 7)
    same_row = row_in == (cols_o & 15)
    band_gap = 32 * ((rows_o >> 5) - ((cols_o >> 4) & 3))
    upper_half = (rows_o >> 3) & 1
    for index in range(S // 2):
        offset = jnp.where(cols_o < 64, offsets[2 * index], offsets[2 * index + 1])
        wrapped = jnp.where(offset > 8 * state, 1, 0)
        chosen = same_row & (band_gap == offset) & (upper_half == wrapped)
        m.spread[:, L * index : L * (index + 1)] = jnp.where(chosen, 1.0, 0.0).astype(BF16)
    for load in loads:
        load.wait()
    for group in range(4):
        m.tg_stage[group] = jnp.concatenate([m.targets_v[:, group, :]] * 4, axis=0)

    pl.semaphore_wait(barrier, T - 1 + 4 * (S - 1))

    def tile_copy(step):
        other = lax.rem(sub + step, 4)
        return pltpu.make_async_remote_copy(
            src_ref=tiles.at[0, 0, pl.ds(R * other, R)],
            dst_ref=m.zb.at[:, pl.ds(pl.multiple_of(32 * sub, 32), 32), :],
            send_sem=m.a_send.at[step],
            recv_sem=m.a_sem,
            device_id=(state, 4 * band + other),
            device_id_type=MESH,
        )

    for step in (2, 3, 1):
        tile_copy(step).start()
    pltpu.make_async_copy(
        tiles.at[0, 0, pl.ds(R * sub, R)],
        m.zb.at[:, pl.ds(pl.multiple_of(32 * sub, 32), 32), :],
        m.a_sem,
    ).start()
    for group in range(4):
        dest = 4 * group + band

        @pl.when(dest != tile)
        def _():
            pltpu.make_async_remote_copy(
                src_ref=m.tg_stage.at[group],
                dst_ref=m.tg_recv.at[sub],
                send_sem=m.tg_send.at[group],
                recv_sem=m.tg_sem,
                device_id=(state, dest),
                device_id_type=MESH,
            ).start()

        @pl.when(dest == tile)
        def _():
            pltpu.make_async_copy(m.tg_stage.at[group], m.tg_recv.at[sub], m.tg_sem).start()

    eye = m.eye[...]
    for index, ref in enumerate((m.wq_v, m.wk_v, m.wv_v, m.wg_v)):
        weight = ref[...]
        m.w_in[:, C * index : C * (index + 1)] = weight
        m.w_in_t[C * index : C * (index + 1), :] = dot_nt(eye, weight).astype(BF16)
    m.wo_t[...] = dot_nt(eye, m.wo_v[...]).astype(BF16)
    head_w = m.wd_v[...]
    high, low = halves(2.0 * head_w)
    m.wd3[...] = jnp.concatenate([high, high, low], axis=1)
    centred = head_w - jnp.mean(head_w, axis=1, keepdims=True)
    high, low = halves(jnp.transpose(centred))
    m.wd_t3[...] = jnp.concatenate([high, high, low], axis=1)
    m.gain_b[...] = column(m.gain_v[...])
    m.lbias_b[...] = column(m.lbias_v[...])
    m.gbias_b[...] = column(m.gbias_v[...])
    m.obias_b[...] = column(m.obias_v[...])
    m.dbias_b[...] = column(m.dbias_v[...])
    for head in range(H):
        m.wpb_b[head] = jnp.broadcast_to(m.wpb_v[:, head : head + 1], (C, L))
    m.dbt[...] = jnp.zeros_like(m.dbt)

    pltpu.make_async_copy(m.zb, m.zb, m.a_sem).wait()

    def norm_row(row, carry):
        z = dot_nt(m.eye[...], m.zb[row])
        centre = z - total(z) * (1.0 / C)
        inverse = lax.rsqrt(total(centre * centre) * (1.0 / C) + 1e-05)
        normed = centre * inverse
        zn = normed * m.gain_b[...] + m.lbias_b[...]
        m.zt[row] = z
        m.xh[row] = normed
        m.inv[row] = inverse
        m.znb[row] = zn.astype(BF16)
        for head in range(H):
            m.b_stage[pl.ds(R * head + row, 1), :] = total(zn * m.wpb_b[head])
        return carry

    lax.fori_loop(0, R, norm_row, 0)

    half = tile // 8
    place = tile % 8
    partner = 8 * (1 - half) + place

    def bias_copy(source, slot, index, sem, dest):
        return pltpu.make_async_remote_copy(
            src_ref=source,
            dst_ref=m.b_recv.at[slot],
            send_sem=m.b_send.at[index],
            recv_sem=m.b_sem.at[sem],
            device_id=(state, dest),
            device_id_type=MESH,
        )

    bias_copy(m.b_stage, tile, 0, 0, partner).start()
    for step in range(1, 8):
        dest = 8 * half + (place + step) % 8
        bias_copy(m.b_stage, tile, step, 1, dest).start()
    pltpu.make_async_copy(m.b_stage, m.b_recv.at[tile], m.b_sem.at[1]).start()

    def project_row(row, carry):
        proj = dot(m.w_in_t[...], m.znb[row])
        keys = proj[C : 2 * C].astype(BF16)
        values = proj[2 * C : 3 * C].astype(BF16)
        queries = proj[:C].astype(BF16)
        m.qt[row] = queries
        m.kt[row] = keys
        m.vt[row] = values
        m.gt[row] = jax.nn.sigmoid(proj[3 * C :] + m.gbias_b[...])
        keys_n = dot_nt(m.eye[...], keys).astype(BF16)
        m.vn[row] = dot_nt(m.eye[...], values).astype(BF16)
        stacked = jnp.concatenate([keys_n * m.hmask[head] for head in range(H)], axis=0)
        m.at[row] = dot(stacked, queries).reshape(H, L, L)
        return carry

    lax.fori_loop(0, R // 2, project_row, 0)

    pltpu.make_async_copy(m.b_stage, m.b_recv.at[partner], m.b_sem.at[0]).wait()
    for step in range(1, 8):
        dest = 8 * half + (place + step) % 8
        bias_copy(m.b_recv.at[partner], partner, 7 + step, 2, dest).start()

    lax.fori_loop(R // 2, R, project_row, 0)

    pltpu.make_async_copy(m.b_recv.at[pl.ds(0, 8)], m.b_recv.at[pl.ds(0, 8)], m.b_sem.at[1]).wait()
    pltpu.make_async_copy(m.b_recv.at[pl.ds(0, 7)], m.b_recv.at[pl.ds(0, 7)], m.b_sem.at[2]).wait()
    for head in range(H):
        rows = jnp.concatenate([m.b_recv[peer, R * head : R * (head + 1), :] for peer in range(T)], axis=0)
        m.bias_t[head] = jnp.transpose(rows) * LOG2E

    def attend_row(row, carry):
        values = m.vt[row]
        parts = []
        for head in range(H):
            scores = m.at[row, head] * (INV_ROOT * LOG2E) + m.bias_t[head]
            top = jnp.max(scores, axis=0, keepdims=True)
            weights = jnp.exp2(scores - top)
            weights = weights * (1.0 / total(weights))
            m.at[row, head] = weights
            parts.append(dot(values[HD * head : HD * (head + 1)], weights.astype(BF16)))
        attended = jnp.concatenate(parts, axis=0)
        m.ot[row] = attended
        gated = (m.gt[row] * attended).astype(BF16)
        updated = m.zt[row] + dot(m.wo_t[...], gated) + m.obias_b[...]
        logits = dot(m.wd_t3[...], three(updated))
        m.lgt[row] = logits
        rounded = logits.astype(BF16)
        start = pl.multiple_of(L * row, L)
        m.lgn[pl.ds(start, L), :] = dot_nt(m.eye[...], jnp.concatenate([rounded, rounded], axis=0))
        return carry

    lax.fori_loop(0, R, attend_row, 0)

    low_lanes = lax.broadcasted_iota(I32, (8, L), 1) < NB

    def logits_out(step, carry):
        dest = lax.rem(tile + step, T)
        parts = []
        for index in range(4):
            first = m.lgn[pl.ds(8 * dest + index, 8, stride=L), :]
            second = m.lgn[pl.ds(8 * dest + 4 + index, 8, stride=L), :]
            parts.append(jnp.where(low_lanes, first, second))
        m.c_stage[dest] = jnp.concatenate(parts, axis=0).astype(BF16)

        @pl.when(step > 0)
        def _():
            pltpu.make_async_remote_copy(
                src_ref=m.c_stage.at[dest],
                dst_ref=m.c_recv.at[tile],
                send_sem=m.c_send.at[step],
                recv_sem=m.c_sem,
                device_id=(state, dest),
                device_id_type=MESH,
            ).start()

        @pl.when(step == 0)
        def _():
            pltpu.make_async_copy(m.c_stage.at[tile], m.c_recv.at[tile], m.c_sem).start()

        return carry

    lax.fori_loop(0, T, logits_out, 0)

    pltpu.make_async_copy(m.tg_recv, m.tg_recv, m.tg_sem).wait()
    pltpu.make_async_copy(m.c_recv, m.c_recv, m.c_sem).wait()

    received = [m.c_recv[peer].astype(F32) for peer in range(T)]
    for index in range(4):
        rows = jnp.concatenate([block[8 * index : 8 * (index + 1)] for block in received], axis=0)
        turned = jnp.transpose(rows)
        m.mirror[index] = turned[:NB]
        m.mirror[4 + index] = turned[NB:]

    bins = lax.broadcasted_iota(I32, (NB, L), 0)

    def backward_row(row, carry):
        logits = m.lgt[row] + m.mirror[row] + m.dbias_b[...]
        top = jnp.max(logits, axis=0, keepdims=True)
        expo = jnp.exp(logits - top)
        prob = expo * (1.0 / total(expo))
        wanted = m.tg_recv[row // 2, pl.ds(lax.rem(row, 2), 1), :]
        residual = prob - jnp.where(bins == wanted, 1.0, 0.0)
        pair_grad = dot(m.wd3[...], three(residual))
        m.dp[row] = pair_grad
        out_grad = dot(m.wo_v[...], pair_grad.astype(BF16))
        gate = m.gt[row]
        gated = out_grad * gate
        att_grad = gated.astype(BF16)
        m.d4[row, 3 * C :] = (gated * m.ot[row] * (1.0 - gate)).astype(BF16)
        values_n = m.vn[row]
        queries = m.qt[row]
        keys = m.kt[row]
        stacked = jnp.concatenate([values_n * m.hmask[head] for head in range(H)], axis=0)
        weight_grad = dot(stacked, att_grad)
        for head in range(H):
            span = slice(HD * head, HD * (head + 1))
            weights = m.at[row, head]
            grads = weight_grad[L * head : L * (head + 1)]
            score = weights * (grads - total(weights * grads))
            m.dbt[head] += score
            score_b = score.astype(BF16)
            m.d4[row, HD * head : HD * (head + 1)] = (dot(keys[span], score_b) * INV_ROOT).astype(BF16)
            m.d4[row, C + HD * head : C + HD * (head + 1)] = (
                dot_nt(queries[span], score_b) * INV_ROOT
            ).astype(BF16)
            m.d4[row, 2 * C + HD * head : 2 * C + HD * (head + 1)] = dot_nt(
                att_grad[span], weights.astype(BF16)
            ).astype(BF16)
        return carry

    lax.fori_loop(0, R, backward_row, 0)

    turned = [jnp.transpose(m.dbt[head]) for head in range(H)]
    for peer in range(T):
        m.e_stage[peer] = jnp.concatenate(
            [block[R * peer : R * (peer + 1)] for block in turned], axis=0
        ).astype(BF16)

    def bias_grad_out(step, carry):
        dest = lax.rem(tile + step, T)
        pltpu.make_async_remote_copy(
            src_ref=m.e_stage.at[dest],
            dst_ref=m.e_recv.at[tile],
            send_sem=m.e_send.at[step],
            recv_sem=m.e_sem,
            device_id=(state, dest),
            device_id_type=MESH,
        ).start()
        return carry

    lax.fori_loop(1, T, bias_grad_out, 0)
    pltpu.make_async_copy(m.e_stage.at[tile], m.e_recv.at[tile], m.e_sem).start()

    def back_project(row, carry):
        m.zt[row] = dot(m.w_in[...], m.d4[row])
        return carry

    lax.fori_loop(0, R, back_project, 0)

    pltpu.make_async_copy(m.e_recv, m.e_recv, m.e_sem).wait()
    bias_sum = m.e_recv[0].astype(F32)
    for peer in range(1, T):
        bias_sum = bias_sum + m.e_recv[peer].astype(F32)
    m.dbs[...] = bias_sum

    def finish_pair(pair, carry):
        for side in range(2):
            row = 2 * pair + side
            zn_grad = m.zt[row]
            for head in range(H):
                zn_grad = zn_grad + m.wpb_b[head] * m.dbs[pl.ds(R * head + row, 1), :]
            scaled = zn_grad * m.gain_b[...]
            normed = m.xh[row]
            mean = total(scaled) * (1.0 / C)
            slope = total(scaled * normed) * (1.0 / C)
            result = m.dp[row] + m.inv[row] * (scaled - mean - normed * slope)
            m.grad[row] = dot_nt(m.shift[...], result.astype(BF16))

        def send_state(step, inner):
            dest = lax.rem(state + step, S)
            start = pl.multiple_of(8 * dest, 8)
            upper = m.grad[2 * pair, pl.ds(start, 8), :]
            lower = m.grad[2 * pair + 1, pl.ds(start, 8), :]
            m.f_stage[pair, dest] = jnp.concatenate([upper, lower], axis=0).astype(BF16)
            target = 4 * sub + pair
            here = jnp.logical_and(step == 0, target == tile)

            @pl.when(jnp.logical_not(here))
            def _():
                pltpu.make_async_remote_copy(
                    src_ref=m.f_stage.at[pair, dest],
                    dst_ref=m.f_recv.at[state, band],
                    send_sem=m.f_send.at[pair, step],
                    recv_sem=m.f_sem,
                    device_id=(dest, target),
                    device_id_type=MESH,
                ).start()

            @pl.when(here)
            def _():
                pltpu.make_async_copy(m.f_stage.at[pair, dest], m.f_recv.at[state, band], m.f_sem).start()

            return inner

        lax.fori_loop(0, S, send_state, 0)
        return carry

    lax.fori_loop(0, 4, finish_pair, 0)

    for step in (2, 3, 1):
        tile_copy(step).wait_send()
    for group in range(4):

        @pl.when(4 * group + band != tile)
        def _():
            pltpu.make_async_copy(m.tg_stage.at[0], m.tg_stage.at[0], m.tg_send.at[group]).wait()

    for index in range(15):
        pltpu.make_async_copy(m.b_stage, m.b_stage, m.b_send.at[index]).wait()

    def sent(step, carry):
        pltpu.make_async_copy(m.c_stage.at[0], m.c_stage.at[0], m.c_send.at[step]).wait()
        pltpu.make_async_copy(m.e_stage.at[0], m.e_stage.at[0], m.e_send.at[step]).wait()
        return carry

    lax.fori_loop(1, T, sent, 0)

    pltpu.make_async_copy(m.f_recv, m.f_recv, m.f_sem).wait()
    out[...] = dot(m.spread[...], m.f_recv[...].reshape(S * 64, C)).reshape(out.shape)

    def sent_state(step, carry):
        for pair in range(4):

            @pl.when(jnp.logical_or(step > 0, 4 * sub + pair != tile))
            def _():
                pltpu.make_async_copy(
                    m.f_stage.at[0, 0], m.f_stage.at[0, 0], m.f_send.at[pair, step]
                ).wait()

        return carry

    lax.fori_loop(0, S, sent_state, 0)


def on_device(
    pair_tiles,
    targets,
    offsets,
    ln_gain,
    ln_bias,
    w_query,
    w_key,
    w_value,
    w_pairbias,
    w_gate,
    gate_bias,
    w_output,
    out_bias,
    w_distogram,
    dist_bias,
):
    anywhere = pl.BlockSpec(memory_space=pl.ANY)
    in_specs = [anywhere] * 15
    in_specs[2] = pl.BlockSpec(memory_space=pltpu.SMEM)
    return pl.pallas_call(
        kernel,
        out_shape=jax.ShapeDtypeStruct((8, 1, 2, 2, L // S, C), F32),
        in_specs=in_specs,
        out_specs=pl.BlockSpec(memory_space=pltpu.VMEM),
        scratch_shapes=list(SCRATCH.values()),
        compiler_params=pltpu.CompilerParams(
            collective_id=0, has_side_effects=True, vmem_limit_bytes=40 * 1024 * 1024
        ),
    )(
        pair_tiles,
        targets,
        offsets,
        ln_gain.reshape(1, C),
        ln_bias.reshape(1, C),
        w_query,
        w_key,
        w_value,
        w_pairbias,
        w_gate,
        gate_bias.reshape(1, C),
        w_output,
        out_bias.reshape(1, C),
        w_distogram,
        dist_bias.reshape(1, NB),
    )


def solution(mesh):
    in_specs = (
        P("state", "tile", None, None, None),
        P("state", "tile", None, None, None),
    ) + (P(),) * 13
    out_specs = P(None, "tile", None, None, "state", None)
    return jax.shard_map(
        on_device, mesh=mesh, in_specs=in_specs, out_specs=out_specs, check_vma=False
    )
```

time: 379 us -> 72.6 us (0.19)
  waiting for transfers between devices: 196 us -> 0 us
  Pallas kernels: 0 us -> 68.6 us
  loops' own time: 36.9 us -> 0 us
  local copies, waits for them, and re-layouts: 36.5 us -> 3.29 us
  blocking collectives: 26.3 us -> 0 us
  matrix products: 24.5 us -> 0 us
  starting transfers between devices: 24.3 us -> 0 us
  between operations: 16.5 us -> 0.17 us
  other arithmetic: 14.6 us -> 0 us
    unnamed x2 -> x0, waiting for transfers between devices: 172 us -> none
    pallas_call x0 -> x1, Pallas kernels: none -> 68.6 us  [on_device(): pl.pallas_call(kernel, out_shape=jax.ShapeDtypeStruct((8, 1, 2, 2, L // S...]
    another operation x3 -> x0, loops' own time: 36.9 us -> none  [the longest x1 36.6 us: on_device(): lax.fori_loop(0, state_count, place, jnp.zeros((full_blocks, row_share, 2...]
    all_gather x1 -> x0, blocking collectives: 26.3 us -> none  [on_device(): gathered = lax.all_gather(bias_rows, 'tile', axis=1, tiled=True)]
    all_to_all x3 -> x0, starting transfers between devices: 24.1 us -> none  [the longest x1 12.6 us: on_device(): lax.all_to_all(blocked, 'tile', split_axis=0, concat_axis=2, tiled=True)]
    all_to_all x3 -> x0, waiting for transfers between devices: 23.4 us -> none  [the longest x1 11.1 us: on_device(): lax.all_to_all(blocked, 'tile', split_axis=0, concat_axis=2, tiled=True)]
    dot_general x38 -> x0, matrix products: 21.4 us -> none  [the longest x4 5.39 us: backward_block(): jnp.einsum('rhjk,rjhd->rkhd', weights_b, grad_blk, preferred_element_type...]
    dynamic_slice x17 -> x0, local copies, waits for them, and re-layouts: 9.85 us -> none  [the longest x16 9.27 us: place(): offset = offsets[source]]
  transfers between devices with their start and end apart: 4 -> 0, of which waited for: 4 -> 0; matrix products, arithmetic and copies ran while one was open for 1% -> 0% of each run, Pallas kernels for 0% -> 0%
where the time goes in v1:
time: 72.6 us; the launch traced here: 72.1 us
  Pallas kernels  68.6 us (94%)
  local copies, waits for them, and re-layouts  3.29 us (5%)
    pallas_call x1, Pallas kernels, on_device(): pl.pallas_call(kernel, out_shape=jax.ShapeDtypeStruct((8, 1, 2, 2, L // S...  68.6 us
    unnamed x31, local copies, waits for them, and re-layouts  3.29 us

profile of v1, /device:TPU:1, one launch (start us, length us, event | category | flops | bytes accessed | tf_op | source)
XLA Modules:
  0.0 72.1 jit_solution(12495798144826582963)
XLA Ops:
  0.0 0.0 copy-start.13
  0.0 0.0 copy-start.10
  0.0 0.0 copy-start.11
  0.0 0.0 copy-start.12
  0.0 0.0 copy-start.6
  0.0 0.7 copy-done.13
  0.7 0.0 copy-start.4
  0.7 0.0 copy-start.5
  0.7 0.0 copy-start.7
  0.7 0.0 copy-start.8
  0.7 0.0 copy-start.9
  0.7 0.1 copy.16.wpb
  0.8 0.0 copy-start.1
  0.8 0.0 copy-start.2
  0.8 0.0 copy-start.3
  0.8 0.9 %copy.17.wd = f32[128,64]{1,0:T(8,128)S(1)} copy(f32[128,64]{0,1:T(8,128)} %param.28) | data formatting | bytes 65536 | tf_op args[13]
  1.7 0.0 copy-done.10
  1.7 0.0 copy-done.11
  1.7 0.0 copy-done.12
  1.7 0.0 copy-done.6
  1.8 0.0 copy-done.4
  1.8 0.0 copy-done.5
  1.8 0.0 copy-done.7
  1.8 0.0 copy-done.8
  1.8 0.0 copy-done.9
  1.8 0.0 copy-done.1
  1.8 0.0 copy-done.2
  1.8 0.0 copy-done.3
  1.8 0.0 copy-start
  1.8 0.9 %copy-done = bf16[1,1,32,32,128]{4,3,2,1,0:T(8,128)(2,1)S(1)} copy-done((bf16[1,1,32,32,128]{4,3,2,1,0:T(8,128)(2,1)S(1)}, bf16[1,1,32,32,128]{4,3,2,1,0:T(8,128)(2,1)}, u32[]{:S(2)}) %copy-start) | copy-done | bytes 262168
  2.8 68.6 %shard_map.145 = f32[8,1,2,2,8,128]{5,4,3,2,1,0:T(8,128)S(1)} custom-call(bf16[1,1,32,32,128]{4,3,2,1,0:T(8,128)(2,1)S(1)} %copy-done, s32[1,1,2,4,128]{4,3,2,1,0:T(4,128)S(1)} %copy-done.6, s32[16]{0:T(128)S(1)} %copy-done.7, f32[1,128]{1,0:T(1,128)S(1)} %bitcast.5, f32[1,128]{1,0:T(1,128)S(1)} %bitcast.6, bf16[128,128]{1,0:T(8,128)(2,1)S(1)} %copy-done.1, ...), custom_call_target="tpu_custom_call" | custom-call | tf_op jit(solution)/shard_map/pallas_call | solution.py:585
  71.4 0.7 copy.19
Async XLA Ops:
  0.0 0.7 copy-start.13
  0.0 1.7 %copy-start.10 = (f32[128]{0:T(128)S(1)}, f32[128]{0:T(128)}, u32[]{:S(2)}) copy-start(f32[128]{0:T(128)} %param.25) | copy-start | bytes 1540
  0.0 1.7 %copy-start.11 = (f32[128]{0:T(128)S(1)}, f32[128]{0:T(128)}, u32[]{:S(2)}) copy-start(f32[128]{0:T(128)} %param.27) | copy-start | bytes 1540
  0.0 1.7 %copy-start.12 = (f32[64]{0:T(128)S(1)}, f32[64]{0:T(128)}, u32[]{:S(2)}) copy-start(f32[64]{0:T(128)} %param.29) | copy-start | bytes 772
  0.0 1.7 %copy-start.6 = (s32[1,1,2,4,128]{4,3,2,1,0:T(4,128)S(1)}, s32[1,1,2,4,128]{4,3,2,1,0:T(4,128)}, u32[]{:S(2)}) copy-start(s32[1,1,2,4,128]{4,3,2,1,0:T(4,128)} %targets.1) | copy-start | bytes 12292
  0.7 1.1 %copy-start.4 = (bf16[128,128]{1,0:T(8,128)(2,1)S(1)}, bf16[128,128]{1,0:T(8,128)(2,1)}, u32[]{:S(2)}) copy-start(bf16[128,128]{1,0:T(8,128)(2,1)} %wg.1) | copy-start | bytes 98308
  0.7 1.1 %copy-start.5 = (bf16[128,128]{1,0:T(8,128)(2,1)S(1)}, bf16[128,128]{1,0:T(8,128)(2,1)}, u32[]{:S(2)}) copy-start(bf16[128,128]{1,0:T(8,128)(2,1)} %wo.1) | copy-start | bytes 98308
  0.7 1.1 %copy-start.7 = (s32[16]{0:T(128)S(1)}, s32[16]{0:T(128)}, u32[]{:S(2)}) copy-start(s32[16]{0:T(128)} %offsets.1) | copy-start | bytes 196
  0.7 1.1 %copy-start.8 = (f32[128]{0:T(128)S(1)}, f32[128]{0:T(128)}, u32[]{:S(2)}) copy-start(f32[128]{0:T(128)} %param.18) | copy-start | bytes 1540
  0.7 1.1 %copy-start.9 = (f32[128]{0:T(128)S(1)}, f32[128]{0:T(128)}, u32[]{:S(2)}) copy-start(f32[128]{0:T(128)} %param.19) | copy-start | bytes 1540
  0.8 1.0 %copy-start.1 = (bf16[128,128]{1,0:T(8,128)(2,1)S(1)}, bf16[128,128]{1,0:T(8,128)(2,1)}, u32[]{:S(2)}) copy-start(bf16[128,128]{1,0:T(8,128)(2,1)} %wq.1) | copy-start | bytes 98308
  0.8 1.0 %copy-start.2 = (bf16[128,128]{1,0:T(8,128)(2,1)S(1)}, bf16[128,128]{1,0:T(8,128)(2,1)}, u32[]{:S(2)}) copy-start(bf16[128,128]{1,0:T(8,128)(2,1)} %wk.1) | copy-start | bytes 98308
  0.8 1.0 %copy-start.3 = (bf16[128,128]{1,0:T(8,128)(2,1)S(1)}, bf16[128,128]{1,0:T(8,128)(2,1)}, u32[]{:S(2)}) copy-start(bf16[128,128]{1,0:T(8,128)(2,1)} %wv.1) | copy-start | bytes 98308
  1.8 1.0 %copy-start = (bf16[1,1,32,32,128]{4,3,2,1,0:T(8,128)(2,1)S(1)}, bf16[1,1,32,32,128]{4,3,2,1,0:T(8,128)(2,1)}, u32[]{:S(2)}) copy-start(bf16[1,1,32,32,128]{4,3,2,1,0:T(8,128)(2,1)} %tiles.1) | copy-start | bytes 786436

commit v2 on v1

--- a/solution.py
+++ b/solution.py
@@ -30,10 +30,10 @@
     wv_v=pltpu.VMEM((C, C), BF16),
     wg_v=pltpu.VMEM((C, C), BF16),
     wo_v=pltpu.VMEM((C, C), BF16),
-    wpb_v=pltpu.VMEM((C, H), F32),
+    wpb_v=pltpu.VMEM((H, C), F32),
     gbias_v=pltpu.VMEM((1, C), F32),
     obias_v=pltpu.VMEM((1, C), F32),
-    wd_v=pltpu.VMEM((C, NB), F32),
+    wd_v=pltpu.VMEM((NB, C), F32),
     dbias_v=pltpu.VMEM((1, NB), F32),
     targets_v=pltpu.VMEM((2, 4, L), I32),
     w_sem=pltpu.SemaphoreType.DMA((13,)),
@@ -69,7 +69,9 @@
     lgn=pltpu.VMEM((R * L, C), F32),
     mirror=pltpu.VMEM((R, NB, L), F32),
     dp=pltpu.VMEM((R, C, L), F32),
-    d4=pltpu.VMEM((R, 4 * C, L), BF16),
+    dgt=pltpu.VMEM((R, C, L), BF16),
+    dot=pltpu.VMEM((R, C, L), BF16),
+    score_b=pltpu.VMEM((R, H, L, L), BF16),
     dbt=pltpu.VMEM((H, L, L), F32),
     dbs=pltpu.VMEM((H * R, L), F32),
     grad=pltpu.VMEM((R, L, C), F32),
@@ -199,6 +201,26 @@
         load.start()
         loads.append(load)
 
+    pl.semaphore_wait(barrier, T - 1 + 4 * (S - 1))
+
+    def tile_copy(step):
+        other = lax.rem(sub + step, 4)
+        return pltpu.make_async_remote_copy(
+            src_ref=tiles.at[0, 0, pl.ds(R * other, R)],
+            dst_ref=m.zb.at[:, pl.ds(pl.multiple_of(32 * sub, 32), 32), :],
+            send_sem=m.a_send.at[step],
+            recv_sem=m.a_sem,
+            device_id=(state, 4 * band + other),
+            device_id_type=MESH,
+        )
+
+    for step in (2, 3, 1):
+        tile_copy(step).start()
+    pltpu.make_async_copy(
+        tiles.at[0, 0, pl.ds(R * sub, R)],
+        m.zb.at[:, pl.ds(pl.multiple_of(32 * sub, 32), 32), :],
+        m.a_sem,
+    ).start()
     rows_i = lax.broadcasted_iota(I32, (C, C), 0)
     cols_i = lax.broadcasted_iota(I32, (C, C), 1)
     m.eye[...] = jnp.where(rows_i == cols_i, 1.0, 0.0).astype(BF16)
@@ -220,27 +242,6 @@
         load.wait()
     for group in range(4):
         m.tg_stage[group] = jnp.concatenate([m.targets_v[:, group, :]] * 4, axis=0)
-
-    pl.semaphore_wait(barrier, T - 1 + 4 * (S - 1))
-
-    def tile_copy(step):
-        other = lax.rem(sub + step, 4)
-        return pltpu.make_async_remote_copy(
-            src_ref=tiles.at[0, 0, pl.ds(R * other, R)],
-            dst_ref=m.zb.at[:, pl.ds(pl.multiple_of(32 * sub, 32), 32), :],
-            send_sem=m.a_send.at[step],
-            recv_sem=m.a_sem,
-            device_id=(state, 4 * band + other),
-            device_id_type=MESH,
-        )
-
-    for step in (2, 3, 1):
-        tile_copy(step).start()
-    pltpu.make_async_copy(
-        tiles.at[0, 0, pl.ds(R * sub, R)],
-        m.zb.at[:, pl.ds(pl.multiple_of(32 * sub, 32), 32), :],
-        m.a_sem,
-    ).start()
     for group in range(4):
         dest = 4 * group + band
 
@@ -266,10 +267,9 @@
         m.w_in_t[C * index : C * (index + 1), :] = dot_nt(eye, weight).astype(BF16)
     m.wo_t[...] = dot_nt(eye, m.wo_v[...]).astype(BF16)
     head_w = m.wd_v[...]
-    high, low = halves(2.0 * head_w)
+    high, low = halves(2.0 * jnp.transpose(head_w))
     m.wd3[...] = jnp.concatenate([high, high, low], axis=1)
-    centred = head_w - jnp.mean(head_w, axis=1, keepdims=True)
-    high, low = halves(jnp.transpose(centred))
+    high, low = halves(head_w - total(head_w) * (1.0 / NB))
     m.wd_t3[...] = jnp.concatenate([high, high, low], axis=1)
     m.gain_b[...] = column(m.gain_v[...])
     m.lbias_b[...] = column(m.lbias_v[...])
@@ -277,7 +277,7 @@
     m.obias_b[...] = column(m.obias_v[...])
     m.dbias_b[...] = column(m.dbias_v[...])
     for head in range(H):
-        m.wpb_b[head] = jnp.broadcast_to(m.wpb_v[:, head : head + 1], (C, L))
+        m.wpb_b[head] = column(m.wpb_v[head : head + 1])
     m.dbt[...] = jnp.zeros_like(m.dbt)
 
     pltpu.make_async_copy(m.zb, m.zb, m.a_sem).wait()
@@ -296,7 +296,7 @@
             m.b_stage[pl.ds(R * head + row, 1), :] = total(zn * m.wpb_b[head])
         return carry
 
-    lax.fori_loop(0, R, norm_row, 0)
+    lax.fori_loop(0, R, norm_row, 0, unroll=True)
 
     half = tile // 8
     place = tile % 8
@@ -333,14 +333,14 @@
         m.at[row] = dot(stacked, queries).reshape(H, L, L)
         return carry
 
-    lax.fori_loop(0, R // 2, project_row, 0)
+    lax.fori_loop(0, R // 2, project_row, 0, unroll=True)
 
     pltpu.make_async_copy(m.b_stage, m.b_recv.at[partner], m.b_sem.at[0]).wait()
     for step in range(1, 8):
         dest = 8 * half + (place + step) % 8
         bias_copy(m.b_recv.at[partner], partner, 7 + step, 2, dest).start()
 
-    lax.fori_loop(R // 2, R, project_row, 0)
+    lax.fori_loop(R // 2, R, project_row, 0, unroll=True)
 
     pltpu.make_async_copy(m.b_recv.at[pl.ds(0, 8)], m.b_recv.at[pl.ds(0, 8)], m.b_sem.at[1]).wait()
     pltpu.make_async_copy(m.b_recv.at[pl.ds(0, 7)], m.b_recv.at[pl.ds(0, 7)], m.b_sem.at[2]).wait()
@@ -369,37 +369,34 @@
         m.lgn[pl.ds(start, L), :] = dot_nt(m.eye[...], jnp.concatenate([rounded, rounded], axis=0))
         return carry
 
-    lax.fori_loop(0, R, attend_row, 0)
+    lax.fori_loop(0, R, attend_row, 0, unroll=True)
+
+    order = [(1, d) for d in (4, 3, 5, 2, 6, 1, 7, 0)] + [(0, d) for d in (4, 3, 5, 2, 6, 1, 7, 0)]
+
+    def peer_of(flip, step):
+        return 8 * (half + flip * (1 - 2 * half)) + (place + step) % 8
 
     low_lanes = lax.broadcasted_iota(I32, (8, L), 1) < NB
 
-    def logits_out(step, carry):
-        dest = lax.rem(tile + step, T)
+    for index, (flip, step) in enumerate(order):
+        dest = peer_of(flip, step)
         parts = []
-        for index in range(4):
-            first = m.lgn[pl.ds(8 * dest + index, 8, stride=L), :]
-            second = m.lgn[pl.ds(8 * dest + 4 + index, 8, stride=L), :]
+        for column_in in range(4):
+            first = m.lgn[pl.ds(8 * dest + column_in, 8, stride=L), :]
+            second = m.lgn[pl.ds(8 * dest + 4 + column_in, 8, stride=L), :]
             parts.append(jnp.where(low_lanes, first, second))
         m.c_stage[dest] = jnp.concatenate(parts, axis=0).astype(BF16)
-
-        @pl.when(step > 0)
-        def _():
+        if index < T - 1:
             pltpu.make_async_remote_copy(
                 src_ref=m.c_stage.at[dest],
                 dst_ref=m.c_recv.at[tile],
-                send_sem=m.c_send.at[step],
+                send_sem=m.c_send.at[index],
                 recv_sem=m.c_sem,
                 device_id=(state, dest),
                 device_id_type=MESH,
             ).start()
-
-        @pl.when(step == 0)
-        def _():
+        else:
             pltpu.make_async_copy(m.c_stage.at[tile], m.c_recv.at[tile], m.c_sem).start()
-
-        return carry
-
-    lax.fori_loop(0, T, logits_out, 0)
 
     pltpu.make_async_copy(m.tg_recv, m.tg_recv, m.tg_sem).wait()
     pltpu.make_async_copy(m.c_recv, m.c_recv, m.c_sem).wait()
@@ -426,10 +423,9 @@
         gate = m.gt[row]
         gated = out_grad * gate
         att_grad = gated.astype(BF16)
-        m.d4[row, 3 * C :] = (gated * m.ot[row] * (1.0 - gate)).astype(BF16)
+        m.dot[row] = att_grad
+        m.dgt[row] = (gated * m.ot[row] * (1.0 - gate)).astype(BF16)
         values_n = m.vn[row]
-        queries = m.qt[row]
-        keys = m.kt[row]
         stacked = jnp.concatenate([values_n * m.hmask[head] for head in range(H)], axis=0)
         weight_grad = dot(stacked, att_grad)
         for head in range(H):
@@ -438,17 +434,10 @@
             grads = weight_grad[L * head : L * (head + 1)]
             score = weights * (grads - total(weights * grads))
             m.dbt[head] += score
-            score_b = score.astype(BF16)
-            m.d4[row, HD * head : HD * (head + 1)] = (dot(keys[span], score_b) * INV_ROOT).astype(BF16)
-            m.d4[row, C + HD * head : C + HD * (head + 1)] = (
-                dot_nt(queries[span], score_b) * INV_ROOT
-            ).astype(BF16)
-            m.d4[row, 2 * C + HD * head : 2 * C + HD * (head + 1)] = dot_nt(
-                att_grad[span], weights.astype(BF16)
-            ).astype(BF16)
-        return carry
-
-    lax.fori_loop(0, R, backward_row, 0)
+            m.score_b[row, head] = score.astype(BF16)
+        return carry
+
+    lax.fori_loop(0, R, backward_row, 0, unroll=True)
 
     turned = [jnp.transpose(m.dbt[head]) for head in range(H)]
     for peer in range(T):
@@ -456,26 +445,32 @@
             [block[R * peer : R * (peer + 1)] for block in turned], axis=0
         ).astype(BF16)
 
-    def bias_grad_out(step, carry):
-        dest = lax.rem(tile + step, T)
+    for index, (flip, step) in enumerate(order[:-1]):
+        dest = peer_of(flip, step)
         pltpu.make_async_remote_copy(
             src_ref=m.e_stage.at[dest],
             dst_ref=m.e_recv.at[tile],
-            send_sem=m.e_send.at[step],
+            send_sem=m.e_send.at[index],
             recv_sem=m.e_sem,
             device_id=(state, dest),
             device_id_type=MESH,
         ).start()
-        return carry
-
-    lax.fori_loop(1, T, bias_grad_out, 0)
     pltpu.make_async_copy(m.e_stage.at[tile], m.e_recv.at[tile], m.e_sem).start()
 
     def back_project(row, carry):
-        m.zt[row] = dot(m.w_in[...], m.d4[row])
-        return carry
-
-    lax.fori_loop(0, R, back_project, 0)
+        queries = m.qt[row]
+        keys = m.kt[row]
+        att_grad = m.dot[row]
+        spans = [slice(HD * head, HD * (head + 1)) for head in range(H)]
+        scores = [m.score_b[row, head] for head in range(H)]
+        parts = [dot(keys[span], score) * INV_ROOT for span, score in zip(spans, scores)]
+        parts += [dot_nt(queries[span], score) * INV_ROOT for span, score in zip(spans, scores)]
+        parts += [dot_nt(att_grad[span], m.at[row, head].astype(BF16)) for head, span in enumerate(spans)]
+        grads = jnp.concatenate(parts, axis=0).astype(BF16)
+        m.zt[row] = dot(m.w_in[...], jnp.concatenate([grads, m.dgt[row]], axis=0))
+        return carry
+
+    lax.fori_loop(0, R, back_project, 0, unroll=True)
 
     pltpu.make_async_copy(m.e_recv, m.e_recv, m.e_sem).wait()
     bias_sum = m.e_recv[0].astype(F32)
@@ -525,7 +520,7 @@
         lax.fori_loop(0, S, send_state, 0)
         return carry
 
-    lax.fori_loop(0, 4, finish_pair, 0)
+    lax.fori_loop(0, 4, finish_pair, 0, unroll=True)
 
     for step in (2, 3, 1):
         tile_copy(step).wait_send()
@@ -543,7 +538,7 @@
         pltpu.make_async_copy(m.e_stage.at[0], m.e_stage.at[0], m.e_send.at[step]).wait()
         return carry
 
-    lax.fori_loop(1, T, sent, 0)
+    lax.fori_loop(0, T - 1, sent, 0)
 
     pltpu.make_async_copy(m.f_recv, m.f_recv, m.f_sem).wait()
     out[...] = dot(m.spread[...], m.f_recv[...].reshape(S * 64, C)).reshape(out.shape)
@@ -579,7 +574,7 @@
     w_distogram,
     dist_bias,
 ):
-    anywhere = pl.BlockSpec(memory_space=pl.ANY)
+    anywhere = pl.BlockSpec(memory_space=pltpu.HBM)
     in_specs = [anywhere] * 15
     in_specs[2] = pl.BlockSpec(memory_space=pltpu.SMEM)
     return pl.pallas_call(
@@ -589,7 +584,7 @@
         out_specs=pl.BlockSpec(memory_space=pltpu.VMEM),
         scratch_shapes=list(SCRATCH.values()),
         compiler_params=pltpu.CompilerParams(
-            collective_id=0, has_side_effects=True, vmem_limit_bytes=40 * 1024 * 1024
+            collective_id=0, has_side_effects=True, vmem_limit_bytes=64 * 1024 * 1024
         ),
     )(
         pair_tiles,
@@ -600,12 +595,12 @@
         w_query,
         w_key,
         w_value,
-        w_pairbias,
+        w_pairbias.T,
         w_gate,
         gate_bias.reshape(1, C),
         w_output,
         out_bias.reshape(1, C),
-        w_distogram,
+        w_distogram.T,
         dist_bias.reshape(1, NB),
     )
 

time: 72.6 us -> 63.2 us (0.87)
  Pallas kernels: 68.6 us -> 61.3 us
  local copies, waits for them, and re-layouts: 3.29 us -> 1.57 us
    pallas_call x1, Pallas kernels: 68.6 us -> 61.3 us  [on_device(): pl.pallas_call(kernel, out_shape=jax.ShapeDtypeStruct((8, 1, 2, 2, L // S...]
    unnamed x31 -> x1, local copies, waits for them, and re-layouts: 3.29 us -> 1.57 us
where the time goes in v2:
time: 63.2 us; the launch traced here: 62.9 us
  Pallas kernels  61.3 us (97%)
  local copies, waits for them, and re-layouts  1.57 us (2%)
    pallas_call x1, Pallas kernels, on_device(): pl.pallas_call(kernel, out_shape=jax.ShapeDtypeStruct((8, 1, 2, 2, L // S...  61.3 us
    unnamed x1, local copies, waits for them, and re-layouts  1.57 us

profile of v2, /device:TPU:1, one launch (start us, length us, event | category | flops | bytes accessed | tf_op | source)
XLA Modules:
  0.0 62.9 jit_solution(14782744973551046167)
XLA Ops:
  0.0 61.3 %shard_map.145 = f32[8,1,2,2,8,128]{5,4,3,2,1,0:T(8,128)} custom-call(bf16[1,1,32,32,128]{4,3,2,1,0:T(8,128)(2,1)} %tiles.1, s32[1,1,2,4,128]{4,3,2,1,0:T(4,128)} %targets.1, s32[16]{0:T(128)} %offsets.1, f32[1,128]{1,0:T(1,128)} %bitcast.9, f32[1,128]{1,0:T(1,128)} %bitcast.10, bf16[128,128]{1,0:T(8,128)(2,1)} %wq.1, bf16[128,128]{1,0:T(8,128)(2,1)} %wk.1, ...), custom_call_target="tpu_custom_call" | custom-call | tf_op jit(solution)/shard_map/pallas_call | solution.py:580
  61.4 1.6 %copy.17 = f32[8,1,2,2,8,128]{5,4,3,2,1,0:T(8,128)} copy(f32[8,1,2,2,8,128]{5,4,3,2,1,0:T(8,128)} %shard_map.145) | data formatting | bytes 262144

commit v3 on v2

--- a/solution.py
+++ b/solution.py
@@ -36,7 +36,7 @@
     wd_v=pltpu.VMEM((NB, C), F32),
     dbias_v=pltpu.VMEM((1, NB), F32),
     targets_v=pltpu.VMEM((2, 4, L), I32),
-    w_sem=pltpu.SemaphoreType.DMA((13,)),
+    w_sem=pltpu.SemaphoreType.DMA((14,)),
     eye=pltpu.VMEM((C, C), BF16),
     hmask=pltpu.VMEM((H, C, C), BF16),
     shift=pltpu.VMEM((L, L), BF16),
@@ -77,8 +77,10 @@
     grad=pltpu.VMEM((R, L, C), F32),
     tg_stage=pltpu.VMEM((4, 8, L), I32),
     tg_recv=pltpu.VMEM((4, 8, L), I32),
-    b_stage=pltpu.VMEM((H * R, L), F32),
-    b_recv=pltpu.VMEM((T, H * R, L), F32),
+    tile_v=pltpu.VMEM((32, 32, C), BF16),
+    b_rows=pltpu.VMEM((H * R, L), F32),
+    b_stage=pltpu.VMEM((32, L), F32),
+    b_recv=pltpu.VMEM((T, 32, L), F32),
     c_stage=pltpu.VMEM((T, 32, L), BF16),
     c_recv=pltpu.VMEM((T, 32, L), BF16),
     e_stage=pltpu.VMEM((T, 32, L), BF16),
@@ -126,6 +128,14 @@
 
 def total(values):
     return jnp.sum(values, axis=0, keepdims=True)
+
+
+def swap(index):
+    return 2 * (index % 2) + index // 2
+
+
+def block_of(device):
+    return device - device % 4 + swap(device % 4)
 
 
 def column(row):
@@ -159,6 +169,8 @@
     tile = lax.axis_index("tile")
     band = tile // 4
     sub = tile % 4
+    group = swap(sub)
+    block = 4 * band + group
 
     barrier = pltpu.get_barrier_semaphore()
 
@@ -171,9 +183,9 @@
 
     def greet_state(step, carry):
         peer = lax.rem(state + step, S)
-        for group in range(4):
+        for index in range(4):
             pl.semaphore_signal(
-                barrier, inc=1, device_id=(peer, 4 * group + band), device_id_type=MESH
+                barrier, inc=1, device_id=(peer, 4 * index + swap(band)), device_id_type=MESH
             )
         return carry
 
@@ -195,18 +207,54 @@
             (wd, m.wd_v),
             (dbias, m.dbias_v),
             (targets.at[0, 0], m.targets_v),
+            (tiles.at[0, 0], m.tile_v),
         ]
     ):
         load = pltpu.make_async_copy(source, target, m.w_sem.at[index])
         load.start()
         loads.append(load)
 
+    rows_i = lax.broadcasted_iota(I32, (C, C), 0)
+    cols_i = lax.broadcasted_iota(I32, (C, C), 1)
+    m.eye[...] = jnp.where(rows_i == cols_i, 1.0, 0.0).astype(BF16)
+    for head in range(H):
+        m.hmask[head] = jnp.where(cols_i // HD == head, 1.0, 0.0).astype(BF16)
+    early = (0, 1, 7, 13)
+    late_loads = [load for index, load in enumerate(loads) if index not in early]
+    for index in early:
+        loads[index].wait()
+    eye = m.eye[...]
+    m.gain_b[...] = column(m.gain_v[...])
+    m.lbias_b[...] = column(m.lbias_v[...])
+    for head in range(H):
+        m.wpb_b[head] = column(m.wpb_v[head : head + 1])
+
+    for index in range(R):
+        z = dot_nt(eye, m.tile_v[4 * index : 4 * (index + 1)].reshape(L, C))
+        centre = z - total(z) * (1.0 / C)
+        inverse = lax.rsqrt(total(centre * centre) * (1.0 / C) + 1e-05)
+        zn = centre * inverse * m.gain_b[...] + m.lbias_b[...]
+        for head in range(H):
+            m.b_rows[R * head + index : R * head + index + 1, :] = total(zn * m.wpb_b[head]) * LOG2E
+    turned = jnp.transpose(m.b_rows[...])
+    rows_s = lax.broadcasted_iota(I32, (32, L), 0)
+    cols_s = lax.broadcasted_iota(I32, (32, L), 1)
+    tile_bias = jnp.zeros((32, L), F32)
+    for part in range(3):
+        piece = turned.astype(BF16)
+        turned = turned - piece.astype(F32)
+        for index in range(4):
+            lane = 32 * (rows_s // R) + 4 * (rows_s % R) + index
+            place_it = jnp.where(lane == cols_s, 1.0, 0.0).astype(BF16)
+            tile_bias = tile_bias + dot(piece[32 * index : 32 * (index + 1)], place_it)
+    m.b_stage[...] = tile_bias
+
     pl.semaphore_wait(barrier, T - 1 + 4 * (S - 1))
 
     def tile_copy(step):
         other = lax.rem(sub + step, 4)
         return pltpu.make_async_remote_copy(
-            src_ref=tiles.at[0, 0, pl.ds(R * other, R)],
+            src_ref=tiles.at[0, 0, pl.ds(R * swap(other), R)],
             dst_ref=m.zb.at[:, pl.ds(pl.multiple_of(32 * sub, 32), 32), :],
             send_sem=m.a_send.at[step],
             recv_sem=m.a_sem,
@@ -214,18 +262,33 @@
             device_id_type=MESH,
         )
 
+    half = tile // 8
+    place = tile % 8
+    partner = 8 * (1 - half) + place
+
+    def bias_copy(source, slot, index, sem, dest):
+        return pltpu.make_async_remote_copy(
+            src_ref=source,
+            dst_ref=m.b_recv.at[slot],
+            send_sem=m.b_send.at[index],
+            recv_sem=m.b_sem.at[sem],
+            device_id=(state, dest),
+            device_id_type=MESH,
+        )
+
+    bias_copy(m.b_stage, tile, 0, 0, partner).start()
     for step in (2, 3, 1):
         tile_copy(step).start()
     pltpu.make_async_copy(
-        tiles.at[0, 0, pl.ds(R * sub, R)],
+        tiles.at[0, 0, pl.ds(R * group, R)],
         m.zb.at[:, pl.ds(pl.multiple_of(32 * sub, 32), 32), :],
         m.a_sem,
     ).start()
-    rows_i = lax.broadcasted_iota(I32, (C, C), 0)
-    cols_i = lax.broadcasted_iota(I32, (C, C), 1)
-    m.eye[...] = jnp.where(rows_i == cols_i, 1.0, 0.0).astype(BF16)
-    for head in range(H):
-        m.hmask[head] = jnp.where(cols_i // HD == head, 1.0, 0.0).astype(BF16)
+    for step in range(1, 8):
+        dest = 8 * half + (place + step) % 8
+        bias_copy(m.b_stage, tile, step, 1, dest).start()
+    pltpu.make_async_copy(m.b_stage, m.b_recv.at[tile], m.b_sem.at[1]).start()
+
     m.shift[...] = jnp.where(((rows_i - offsets[state] + L) & (L - 1)) == cols_i, 1.0, 0.0).astype(BF16)
     rows_o = lax.broadcasted_iota(I32, (256, L), 0)
     cols_o = lax.broadcasted_iota(I32, (256, L), 1)
@@ -238,19 +301,19 @@
         wrapped = jnp.where(offset > 8 * state, 1, 0)
         chosen = same_row & (band_gap == offset) & (upper_half == wrapped)
         m.spread[:, L * index : L * (index + 1)] = jnp.where(chosen, 1.0, 0.0).astype(BF16)
-    for load in loads:
+    for load in late_loads:
         load.wait()
-    for group in range(4):
-        m.tg_stage[group] = jnp.concatenate([m.targets_v[:, group, :]] * 4, axis=0)
-    for group in range(4):
-        dest = 4 * group + band
+    for index in range(4):
+        m.tg_stage[index] = jnp.concatenate([m.targets_v[:, index, :]] * 4, axis=0)
+    for index in range(4):
+        dest = 4 * index + swap(band)
 
         @pl.when(dest != tile)
         def _():
             pltpu.make_async_remote_copy(
-                src_ref=m.tg_stage.at[group],
+                src_ref=m.tg_stage.at[index],
                 dst_ref=m.tg_recv.at[sub],
-                send_sem=m.tg_send.at[group],
+                send_sem=m.tg_send.at[index],
                 recv_sem=m.tg_sem,
                 device_id=(state, dest),
                 device_id_type=MESH,
@@ -258,9 +321,8 @@
 
         @pl.when(dest == tile)
         def _():
-            pltpu.make_async_copy(m.tg_stage.at[group], m.tg_recv.at[sub], m.tg_sem).start()
-
-    eye = m.eye[...]
+            pltpu.make_async_copy(m.tg_stage.at[index], m.tg_recv.at[sub], m.tg_sem).start()
+
     for index, ref in enumerate((m.wq_v, m.wk_v, m.wv_v, m.wg_v)):
         weight = ref[...]
         m.w_in[:, C * index : C * (index + 1)] = weight
@@ -271,13 +333,9 @@
     m.wd3[...] = jnp.concatenate([high, high, low], axis=1)
     high, low = halves(head_w - total(head_w) * (1.0 / NB))
     m.wd_t3[...] = jnp.concatenate([high, high, low], axis=1)
-    m.gain_b[...] = column(m.gain_v[...])
-    m.lbias_b[...] = column(m.lbias_v[...])
     m.gbias_b[...] = column(m.gbias_v[...])
     m.obias_b[...] = column(m.obias_v[...])
     m.dbias_b[...] = column(m.dbias_v[...])
-    for head in range(H):
-        m.wpb_b[head] = column(m.wpb_v[head : head + 1])
     m.dbt[...] = jnp.zeros_like(m.dbt)
 
     pltpu.make_async_copy(m.zb, m.zb, m.a_sem).wait()
@@ -292,31 +350,9 @@
         m.xh[row] = normed
         m.inv[row] = inverse
         m.znb[row] = zn.astype(BF16)
-        for head in range(H):
-            m.b_stage[pl.ds(R * head + row, 1), :] = total(zn * m.wpb_b[head])
         return carry
 
     lax.fori_loop(0, R, norm_row, 0, unroll=True)
-
-    half = tile // 8
-    place = tile % 8
-    partner = 8 * (1 - half) + place
-
-    def bias_copy(source, slot, index, sem, dest):
-        return pltpu.make_async_remote_copy(
-            src_ref=source,
-            dst_ref=m.b_recv.at[slot],
-            send_sem=m.b_send.at[index],
-            recv_sem=m.b_sem.at[sem],
-            device_id=(state, dest),
-            device_id_type=MESH,
-        )
-
-    bias_copy(m.b_stage, tile, 0, 0, partner).start()
-    for step in range(1, 8):
-        dest = 8 * half + (place + step) % 8
-        bias_copy(m.b_stage, tile, step, 1, dest).start()
-    pltpu.make_async_copy(m.b_stage, m.b_recv.at[tile], m.b_sem.at[1]).start()
 
     def project_row(row, carry):
         proj = dot(m.w_in_t[...], m.znb[row])
@@ -333,20 +369,18 @@
         m.at[row] = dot(stacked, queries).reshape(H, L, L)
         return carry
 
-    lax.fori_loop(0, R // 2, project_row, 0, unroll=True)
-
     pltpu.make_async_copy(m.b_stage, m.b_recv.at[partner], m.b_sem.at[0]).wait()
     for step in range(1, 8):
         dest = 8 * half + (place + step) % 8
         bias_copy(m.b_recv.at[partner], partner, 7 + step, 2, dest).start()
 
-    lax.fori_loop(R // 2, R, project_row, 0, unroll=True)
+    lax.fori_loop(0, R, project_row, 0, unroll=True)
 
     pltpu.make_async_copy(m.b_recv.at[pl.ds(0, 8)], m.b_recv.at[pl.ds(0, 8)], m.b_sem.at[1]).wait()
     pltpu.make_async_copy(m.b_recv.at[pl.ds(0, 7)], m.b_recv.at[pl.ds(0, 7)], m.b_sem.at[2]).wait()
+    bands = [m.b_recv[4 * index : 4 * (index + 1)].reshape(L, L) for index in range(4)]
     for head in range(H):
-        rows = jnp.concatenate([m.b_recv[peer, R * head : R * (head + 1), :] for peer in range(T)], axis=0)
-        m.bias_t[head] = jnp.transpose(rows) * LOG2E
+        m.bias_t[head] = jnp.concatenate([part[:, 32 * head : 32 * (head + 1)] for part in bands], axis=1)
 
     def attend_row(row, carry):
         values = m.vt[row]
@@ -380,23 +414,24 @@
 
     for index, (flip, step) in enumerate(order):
         dest = peer_of(flip, step)
+        theirs = block_of(dest)
         parts = []
         for column_in in range(4):
-            first = m.lgn[pl.ds(8 * dest + column_in, 8, stride=L), :]
-            second = m.lgn[pl.ds(8 * dest + 4 + column_in, 8, stride=L), :]
+            first = m.lgn[pl.ds(8 * theirs + column_in, 8, stride=L), :]
+            second = m.lgn[pl.ds(8 * theirs + 4 + column_in, 8, stride=L), :]
             parts.append(jnp.where(low_lanes, first, second))
-        m.c_stage[dest] = jnp.concatenate(parts, axis=0).astype(BF16)
+        m.c_stage[theirs] = jnp.concatenate(parts, axis=0).astype(BF16)
         if index < T - 1:
             pltpu.make_async_remote_copy(
-                src_ref=m.c_stage.at[dest],
-                dst_ref=m.c_recv.at[tile],
+                src_ref=m.c_stage.at[theirs],
+                dst_ref=m.c_recv.at[block],
                 send_sem=m.c_send.at[index],
                 recv_sem=m.c_sem,
                 device_id=(state, dest),
                 device_id_type=MESH,
             ).start()
         else:
-            pltpu.make_async_copy(m.c_stage.at[tile], m.c_recv.at[tile], m.c_sem).start()
+            pltpu.make_async_copy(m.c_stage.at[block], m.c_recv.at[block], m.c_sem).start()
 
     pltpu.make_async_copy(m.tg_recv, m.tg_recv, m.tg_sem).wait()
     pltpu.make_async_copy(m.c_recv, m.c_recv, m.c_sem).wait()
@@ -448,14 +483,14 @@
     for index, (flip, step) in enumerate(order[:-1]):
         dest = peer_of(flip, step)
         pltpu.make_async_remote_copy(
-            src_ref=m.e_stage.at[dest],
-            dst_ref=m.e_recv.at[tile],
+            src_ref=m.e_stage.at[block_of(dest)],
+            dst_ref=m.e_recv.at[block],
             send_sem=m.e_send.at[index],
             recv_sem=m.e_sem,
             device_id=(state, dest),
             device_id_type=MESH,
         ).start()
-    pltpu.make_async_copy(m.e_stage.at[tile], m.e_recv.at[tile], m.e_sem).start()
+    pltpu.make_async_copy(m.e_stage.at[block], m.e_recv.at[block], m.e_sem).start()
 
     def back_project(row, carry):
         queries = m.qt[row]
@@ -491,17 +526,15 @@
             result = m.dp[row] + m.inv[row] * (scaled - mean - normed * slope)
             m.grad[row] = dot_nt(m.shift[...], result.astype(BF16))
 
-        def send_state(step, inner):
-            dest = lax.rem(state + step, S)
+        target = 4 * group + pair
+        for step, (dy, dz) in enumerate(state_order):
+            dest = 4 * lax.rem(state // 4 + dy, 4) + lax.rem(state % 4 + dz, 4)
             start = pl.multiple_of(8 * dest, 8)
             upper = m.grad[2 * pair, pl.ds(start, 8), :]
             lower = m.grad[2 * pair + 1, pl.ds(start, 8), :]
             m.f_stage[pair, dest] = jnp.concatenate([upper, lower], axis=0).astype(BF16)
-            target = 4 * sub + pair
-            here = jnp.logical_and(step == 0, target == tile)
-
-            @pl.when(jnp.logical_not(here))
-            def _():
+
+            def send(dest=dest, step=step):
                 pltpu.make_async_remote_copy(
                     src_ref=m.f_stage.at[pair, dest],
                     dst_ref=m.f_recv.at[state, band],
@@ -511,24 +544,29 @@
                     device_id_type=MESH,
                 ).start()
 
-            @pl.when(here)
-            def _():
-                pltpu.make_async_copy(m.f_stage.at[pair, dest], m.f_recv.at[state, band], m.f_sem).start()
-
-            return inner
-
-        lax.fori_loop(0, S, send_state, 0)
-        return carry
-
+            if step < S - 1:
+                send()
+            else:
+                pl.when(target != tile)(send)
+
+                @pl.when(target == tile)
+                def _():
+                    pltpu.make_async_copy(
+                        m.f_stage.at[pair, state], m.f_recv.at[state, band], m.f_sem
+                    ).start()
+
+        return carry
+
+    state_order = [(dy, dz) for dy in (2, 1, 3, 0) for dz in (2, 1, 3, 0)]
     lax.fori_loop(0, 4, finish_pair, 0, unroll=True)
 
     for step in (2, 3, 1):
         tile_copy(step).wait_send()
-    for group in range(4):
-
-        @pl.when(4 * group + band != tile)
+    for index in range(4):
+
+        @pl.when(4 * index + swap(band) != tile)
         def _():
-            pltpu.make_async_copy(m.tg_stage.at[0], m.tg_stage.at[0], m.tg_send.at[group]).wait()
+            pltpu.make_async_copy(m.tg_stage.at[0], m.tg_stage.at[0], m.tg_send.at[index]).wait()
 
     for index in range(15):
         pltpu.make_async_copy(m.b_stage, m.b_stage, m.b_send.at[index]).wait()
@@ -546,7 +584,7 @@
     def sent_state(step, carry):
         for pair in range(4):
 
-            @pl.when(jnp.logical_or(step > 0, 4 * sub + pair != tile))
+            @pl.when(jnp.logical_or(step < S - 1, 4 * group + pair != tile))
             def _():
                 pltpu.make_async_copy(
                     m.f_stage.at[0, 0], m.f_stage.at[0, 0], m.f_send.at[pair, step]

time: 63.2 us -> 54.6 us (0.86)
  Pallas kernels: 61.3 us -> 52.9 us
    pallas_call x1, Pallas kernels: 61.3 us -> 52.9 us  [on_device(): pl.pallas_call(kernel, out_shape=jax.ShapeDtypeStruct((8, 1, 2, 2, L // S...]
where the time goes in v3:
time: 54.6 us; the launch traced here: 54.5 us
  Pallas kernels  52.9 us (97%)
  local copies, waits for them, and re-layouts  1.57 us (3%)
    pallas_call x1, Pallas kernels, on_device(): pl.pallas_call(kernel, out_shape=jax.ShapeDtypeStruct((8, 1, 2, 2, L // S...  52.9 us
    unnamed x1, local copies, waits for them, and re-layouts  1.57 us

profile of v3, /device:TPU:1, one launch (start us, length us, event | category | flops | bytes accessed | tf_op | source)
XLA Modules:
  0.0 54.5 jit_solution(8528778384941847988)
XLA Ops:
  0.0 52.9 %shard_map.145 = f32[8,1,2,2,8,128]{5,4,3,2,1,0:T(8,128)} custom-call(bf16[1,1,32,32,128]{4,3,2,1,0:T(8,128)(2,1)} %tiles.1, s32[1,1,2,4,128]{4,3,2,1,0:T(4,128)} %targets.1, s32[16]{0:T(128)} %offsets.1, f32[1,128]{1,0:T(1,128)} %bitcast.9, f32[1,128]{1,0:T(1,128)} %bitcast.10, bf16[128,128]{1,0:T(8,128)(2,1)} %wq.1, bf16[128,128]{1,0:T(8,128)(2,1)} %wk.1, ...), custom_call_target="tpu_custom_call" | custom-call | tf_op jit(solution)/shard_map/pallas_call | solution.py:618
  53.0 1.6 %copy.17 = f32[8,1,2,2,8,128]{5,4,3,2,1,0:T(8,128)} copy(f32[8,1,2,2,8,128]{5,4,3,2,1,0:T(8,128)} %shard_map.145) | data formatting | bytes 262144

commit v4 on v3

--- a/solution.py
+++ b/solution.py
@@ -354,27 +354,27 @@
 
     lax.fori_loop(0, R, norm_row, 0, unroll=True)
 
-    def project_row(row, carry):
-        proj = dot(m.w_in_t[...], m.znb[row])
-        keys = proj[C : 2 * C].astype(BF16)
-        values = proj[2 * C : 3 * C].astype(BF16)
-        queries = proj[:C].astype(BF16)
-        m.qt[row] = queries
-        m.kt[row] = keys
-        m.vt[row] = values
-        m.gt[row] = jax.nn.sigmoid(proj[3 * C :] + m.gbias_b[...])
-        keys_n = dot_nt(m.eye[...], keys).astype(BF16)
-        m.vn[row] = dot_nt(m.eye[...], values).astype(BF16)
-        stacked = jnp.concatenate([keys_n * m.hmask[head] for head in range(H)], axis=0)
-        m.at[row] = dot(stacked, queries).reshape(H, L, L)
-        return carry
-
     pltpu.make_async_copy(m.b_stage, m.b_recv.at[partner], m.b_sem.at[0]).wait()
     for step in range(1, 8):
         dest = 8 * half + (place + step) % 8
         bias_copy(m.b_recv.at[partner], partner, 7 + step, 2, dest).start()
 
-    lax.fori_loop(0, R, project_row, 0, unroll=True)
+    for row in range(0, R, 2):
+        proj = dot(m.w_in_t[...], jnp.concatenate([m.znb[row], m.znb[row + 1]], axis=1))
+        queries_keys_values = proj[: 3 * C].astype(BF16)
+        gates = proj[3 * C :]
+        for side in range(2):
+            here = row + side
+            span = slice(L * side, L * (side + 1))
+            m.qt[here] = queries_keys_values[:C, span]
+            m.kt[here] = queries_keys_values[C : 2 * C, span]
+            m.vt[here] = queries_keys_values[2 * C :, span]
+            m.gt[here] = jax.nn.sigmoid(gates[:, span] + m.gbias_b[...])
+            natural = dot_nt(m.eye[...], queries_keys_values[C:, span]).astype(BF16)
+            m.vn[here] = natural[:, C:]
+            stacked = jnp.concatenate([natural[:, :C] * m.hmask[head] for head in range(H)], axis=0)
+            scores = dot(stacked, queries_keys_values[:C, span]) * (INV_ROOT * LOG2E)
+            m.at[here] = scores.reshape(H, L, L)
 
     pltpu.make_async_copy(m.b_recv.at[pl.ds(0, 8)], m.b_recv.at[pl.ds(0, 8)], m.b_sem.at[1]).wait()
     pltpu.make_async_copy(m.b_recv.at[pl.ds(0, 7)], m.b_recv.at[pl.ds(0, 7)], m.b_sem.at[2]).wait()
@@ -382,11 +382,11 @@
     for head in range(H):
         m.bias_t[head] = jnp.concatenate([part[:, 32 * head : 32 * (head + 1)] for part in bands], axis=1)
 
-    def attend_row(row, carry):
+    def attend(row):
         values = m.vt[row]
         parts = []
         for head in range(H):
-            scores = m.at[row, head] * (INV_ROOT * LOG2E) + m.bias_t[head]
+            scores = m.at[row, head] + m.bias_t[head]
             top = jnp.max(scores, axis=0, keepdims=True)
             weights = jnp.exp2(scores - top)
             weights = weights * (1.0 / total(weights))
@@ -394,16 +394,27 @@
             parts.append(dot(values[HD * head : HD * (head + 1)], weights.astype(BF16)))
         attended = jnp.concatenate(parts, axis=0)
         m.ot[row] = attended
-        gated = (m.gt[row] * attended).astype(BF16)
-        updated = m.zt[row] + dot(m.wo_t[...], gated) + m.obias_b[...]
+        return (m.gt[row] * attended).astype(BF16)
+
+    def predict(row, gated):
+        added = dot(m.wo_t[...], jnp.concatenate(gated, axis=1))
+        updated = jnp.concatenate([m.zt[row] + m.obias_b[...], m.zt[row + 1] + m.obias_b[...]], axis=1) + added
         logits = dot(m.wd_t3[...], three(updated))
-        m.lgt[row] = logits
+        m.lgt[row] = logits[:, :L]
+        m.lgt[row + 1] = logits[:, L:]
         rounded = logits.astype(BF16)
-        start = pl.multiple_of(L * row, L)
-        m.lgn[pl.ds(start, L), :] = dot_nt(m.eye[...], jnp.concatenate([rounded, rounded], axis=0))
-        return carry
-
-    lax.fori_loop(0, R, attend_row, 0, unroll=True)
+        first, second = rounded[:, :L], rounded[:, L:]
+        turned = dot_nt(m.eye[...], jnp.concatenate([first, first, second, second], axis=0))
+        m.lgn[L * row : L * (row + 1), :] = turned[:, :C]
+        m.lgn[L * (row + 1) : L * (row + 2), :] = turned[:, C:]
+
+    waiting = None
+    for row in range(0, R, 2):
+        gated = [attend(row), attend(row + 1)]
+        if waiting is not None:
+            predict(*waiting)
+        waiting = (row, gated)
+    predict(*waiting)
 
     order = [(1, d) for d in (4, 3, 5, 2, 6, 1, 7, 0)] + [(0, d) for d in (4, 3, 5, 2, 6, 1, 7, 0)]
 
@@ -445,16 +456,21 @@
 
     bins = lax.broadcasted_iota(I32, (NB, L), 0)
 
-    def backward_row(row, carry):
+    def residual(row):
         logits = m.lgt[row] + m.mirror[row] + m.dbias_b[...]
         top = jnp.max(logits, axis=0, keepdims=True)
         expo = jnp.exp(logits - top)
         prob = expo * (1.0 / total(expo))
-        wanted = m.tg_recv[row // 2, pl.ds(lax.rem(row, 2), 1), :]
-        residual = prob - jnp.where(bins == wanted, 1.0, 0.0)
-        pair_grad = dot(m.wd3[...], three(residual))
-        m.dp[row] = pair_grad
-        out_grad = dot(m.wo_v[...], pair_grad.astype(BF16))
+        wanted = m.tg_recv[row // 2, row % 2 : row % 2 + 1, :]
+        return prob - jnp.where(bins == wanted, 1.0, 0.0)
+
+    def out_gradient(row):
+        pair_grad = dot(m.wd3[...], three(jnp.concatenate([residual(row), residual(row + 1)], axis=1)))
+        m.dp[row] = pair_grad[:, :L]
+        m.dp[row + 1] = pair_grad[:, L:]
+        return dot(m.wo_v[...], pair_grad.astype(BF16))
+
+    def score_gradient(row, out_grad):
         gate = m.gt[row]
         gated = out_grad * gate
         att_grad = gated.astype(BF16)
@@ -464,15 +480,19 @@
         stacked = jnp.concatenate([values_n * m.hmask[head] for head in range(H)], axis=0)
         weight_grad = dot(stacked, att_grad)
         for head in range(H):
-            span = slice(HD * head, HD * (head + 1))
             weights = m.at[row, head]
             grads = weight_grad[L * head : L * (head + 1)]
             score = weights * (grads - total(weights * grads))
             m.dbt[head] += score
             m.score_b[row, head] = score.astype(BF16)
-        return carry
-
-    lax.fori_loop(0, R, backward_row, 0, unroll=True)
+
+    grads = out_gradient(0)
+    for row in range(0, R, 2):
+        current = grads
+        if row + 2 < R:
+            grads = out_gradient(row + 2)
+        score_gradient(row, current[:, :L])
+        score_gradient(row + 1, current[:, L:])
 
     turned = [jnp.transpose(m.dbt[head]) for head in range(H)]
     for peer in range(T):
@@ -492,7 +512,7 @@
         ).start()
     pltpu.make_async_copy(m.e_stage.at[block], m.e_recv.at[block], m.e_sem).start()
 
-    def back_project(row, carry):
+    def projections(row):
         queries = m.qt[row]
         keys = m.kt[row]
         att_grad = m.dot[row]
@@ -501,11 +521,12 @@
         parts = [dot(keys[span], score) * INV_ROOT for span, score in zip(spans, scores)]
         parts += [dot_nt(queries[span], score) * INV_ROOT for span, score in zip(spans, scores)]
         parts += [dot_nt(att_grad[span], m.at[row, head].astype(BF16)) for head, span in enumerate(spans)]
-        grads = jnp.concatenate(parts, axis=0).astype(BF16)
-        m.zt[row] = dot(m.w_in[...], jnp.concatenate([grads, m.dgt[row]], axis=0))
-        return carry
-
-    lax.fori_loop(0, R, back_project, 0, unroll=True)
+        return jnp.concatenate([jnp.concatenate(parts, axis=0).astype(BF16), m.dgt[row]], axis=0)
+
+    for row in range(0, R, 2):
+        both = dot(m.w_in[...], jnp.concatenate([projections(row), projections(row + 1)], axis=1))
+        m.zt[row] = both[:, :L]
+        m.zt[row + 1] = both[:, L:]
 
     pltpu.make_async_copy(m.e_recv, m.e_recv, m.e_sem).wait()
     bias_sum = m.e_recv[0].astype(F32)

time: 54.6 us -> 52 us (0.952)
  Pallas kernels: 52.9 us -> 50.3 us
    pallas_call x1, Pallas kernels: 52.9 us -> 50.3 us  [on_device(): pl.pallas_call(kernel, out_shape=jax.ShapeDtypeStruct((8, 1, 2, 2, L // S...]
where the time goes in v4:
time: 52 us; the launch traced here: 51.9 us
  Pallas kernels  50.3 us (97%)
  local copies, waits for them, and re-layouts  1.57 us (3%)
    pallas_call x1, Pallas kernels, on_device(): pl.pallas_call(kernel, out_shape=jax.ShapeDtypeStruct((8, 1, 2, 2, L // S...  50.3 us
    unnamed x1, local copies, waits for them, and re-layouts  1.57 us

profile of v4, /device:TPU:1, one launch (start us, length us, event | category | flops | bytes accessed | tf_op | source)
XLA Modules:
  0.0 51.9 jit_solution(16406590998998375651)
XLA Ops:
  0.0 50.3 %shard_map.145 = f32[8,1,2,2,8,128]{5,4,3,2,1,0:T(8,128)} custom-call(bf16[1,1,32,32,128]{4,3,2,1,0:T(8,128)(2,1)} %tiles.1, s32[1,1,2,4,128]{4,3,2,1,0:T(4,128)} %targets.1, s32[16]{0:T(128)} %offsets.1, f32[1,128]{1,0:T(1,128)} %bitcast.9, f32[1,128]{1,0:T(1,128)} %bitcast.10, bf16[128,128]{1,0:T(8,128)(2,1)} %wq.1, bf16[128,128]{1,0:T(8,128)(2,1)} %wk.1, ...), custom_call_target="tpu_custom_call" | custom-call | tf_op jit(solution)/shard_map/pallas_call | solution.py:639
  50.3 1.6 %copy.17 = f32[8,1,2,2,8,128]{5,4,3,2,1,0:T(8,128)} copy(f32[8,1,2,2,8,128]{5,4,3,2,1,0:T(8,128)} %shard_map.145) | data formatting | bytes 262144

commit v5 on v4

--- a/solution.py
+++ b/solution.py
@@ -36,7 +36,8 @@
     wd_v=pltpu.VMEM((NB, C), F32),
     dbias_v=pltpu.VMEM((1, NB), F32),
     targets_v=pltpu.VMEM((2, 4, L), I32),
-    w_sem=pltpu.SemaphoreType.DMA((14,)),
+    offsets_s=pltpu.SMEM((S,), I32),
+    w_sem=pltpu.SemaphoreType.DMA((15,)),
     eye=pltpu.VMEM((C, C), BF16),
     hmask=pltpu.VMEM((H, C, C), BF16),
     shift=pltpu.VMEM((L, L), BF16),
@@ -208,6 +209,7 @@
             (dbias, m.dbias_v),
             (targets.at[0, 0], m.targets_v),
             (tiles.at[0, 0], m.tile_v),
+            (offsets, m.offsets_s),
         ]
     ):
         load = pltpu.make_async_copy(source, target, m.w_sem.at[index])
@@ -289,7 +291,9 @@
         bias_copy(m.b_stage, tile, step, 1, dest).start()
     pltpu.make_async_copy(m.b_stage, m.b_recv.at[tile], m.b_sem.at[1]).start()
 
-    m.shift[...] = jnp.where(((rows_i - offsets[state] + L) & (L - 1)) == cols_i, 1.0, 0.0).astype(BF16)
+    for load in late_loads:
+        load.wait()
+    m.shift[...] = jnp.where(((rows_i - m.offsets_s[state] + L) & (L - 1)) == cols_i, 1.0, 0.0).astype(BF16)
     rows_o = lax.broadcasted_iota(I32, (256, L), 0)
     cols_o = lax.broadcasted_iota(I32, (256, L), 1)
     row_in = 8 * ((rows_o >> 4) & 1) + (rows_o & 7)
@@ -297,12 +301,10 @@
     band_gap = 32 * ((rows_o >> 5) - ((cols_o >> 4) & 3))
     upper_half = (rows_o >> 3) & 1
     for index in range(S // 2):
-        offset = jnp.where(cols_o < 64, offsets[2 * index], offsets[2 * index + 1])
+        offset = jnp.where(cols_o < 64, m.offsets_s[2 * index], m.offsets_s[2 * index + 1])
         wrapped = jnp.where(offset > 8 * state, 1, 0)
         chosen = same_row & (band_gap == offset) & (upper_half == wrapped)
         m.spread[:, L * index : L * (index + 1)] = jnp.where(chosen, 1.0, 0.0).astype(BF16)
-    for load in late_loads:
-        load.wait()
     for index in range(4):
         m.tg_stage[index] = jnp.concatenate([m.targets_v[:, index, :]] * 4, axis=0)
     for index in range(4):
@@ -336,7 +338,6 @@
     m.gbias_b[...] = column(m.gbias_v[...])
     m.obias_b[...] = column(m.obias_v[...])
     m.dbias_b[...] = column(m.dbias_v[...])
-    m.dbt[...] = jnp.zeros_like(m.dbt)
 
     pltpu.make_async_copy(m.zb, m.zb, m.a_sem).wait()
 
@@ -470,29 +471,35 @@
         m.dp[row + 1] = pair_grad[:, L:]
         return dot(m.wo_v[...], pair_grad.astype(BF16))
 
-    def score_gradient(row, out_grad):
-        gate = m.gt[row]
-        gated = out_grad * gate
-        att_grad = gated.astype(BF16)
-        m.dot[row] = att_grad
-        m.dgt[row] = (gated * m.ot[row] * (1.0 - gate)).astype(BF16)
-        values_n = m.vn[row]
-        stacked = jnp.concatenate([values_n * m.hmask[head] for head in range(H)], axis=0)
-        weight_grad = dot(stacked, att_grad)
+    def score_gradients(row, out_grad):
+        weight_grads = []
+        for side in range(2):
+            here = row + side
+            gate = m.gt[here]
+            gated = out_grad[:, L * side : L * (side + 1)] * gate
+            att_grad = gated.astype(BF16)
+            m.dot[here] = att_grad
+            m.dgt[here] = (gated * m.ot[here] * (1.0 - gate)).astype(BF16)
+            values_n = m.vn[here]
+            stacked = jnp.concatenate([values_n * m.hmask[head] for head in range(H)], axis=0)
+            weight_grads.append(dot(stacked, att_grad))
         for head in range(H):
-            weights = m.at[row, head]
-            grads = weight_grad[L * head : L * (head + 1)]
-            score = weights * (grads - total(weights * grads))
-            m.dbt[head] += score
-            m.score_b[row, head] = score.astype(BF16)
+            scores = []
+            for side in range(2):
+                weights = m.at[row + side, head]
+                grads = weight_grads[side][L * head : L * (head + 1)]
+                score = weights * (grads - total(weights * grads))
+                m.score_b[row + side, head] = score.astype(BF16)
+                scores.append(score)
+            both = scores[0] + scores[1]
+            m.dbt[head] = both if row == 0 else m.dbt[head] + both
 
     grads = out_gradient(0)
     for row in range(0, R, 2):
         current = grads
         if row + 2 < R:
             grads = out_gradient(row + 2)
-        score_gradient(row, current[:, :L])
-        score_gradient(row + 1, current[:, L:])
+        score_gradients(row, current)
 
     turned = [jnp.transpose(m.dbt[head]) for head in range(H)]
     for peer in range(T):
@@ -635,17 +642,17 @@
 ):
     anywhere = pl.BlockSpec(memory_space=pltpu.HBM)
     in_specs = [anywhere] * 15
-    in_specs[2] = pl.BlockSpec(memory_space=pltpu.SMEM)
-    return pl.pallas_call(
+    call = pl.pallas_call(
         kernel,
         out_shape=jax.ShapeDtypeStruct((8, 1, 2, 2, L // S, C), F32),
         in_specs=in_specs,
         out_specs=pl.BlockSpec(memory_space=pltpu.VMEM),
         scratch_shapes=list(SCRATCH.values()),
         compiler_params=pltpu.CompilerParams(
-            collective_id=0, has_side_effects=True, vmem_limit_bytes=64 * 1024 * 1024
+            collective_id=0, has_side_effects=True, vmem_limit_bytes=52 * 1024 * 1024
         ),
-    )(
+    )
+    operands = (
         pair_tiles,
         targets,
         offsets,
@@ -662,6 +669,10 @@
         w_distogram.T,
         dist_bias.reshape(1, NB),
     )
+    operands = [
+        pltpu.with_memory_space_constraint(operand, pltpu.HBM) for operand in operands
+    ]
+    return call(*operands)
 
 
 def solution(mesh):

time: 52 us -> 49.6 us (0.954)
  Pallas kernels: 50.3 us -> 48.8 us
  local copies, waits for them, and re-layouts: 1.57 us -> 0.66 us
    pallas_call x1, Pallas kernels: 50.3 us -> 48.8 us  [on_device(): return call(*operands)]
    unnamed x1, local copies, waits for them, and re-layouts: 1.57 us -> 0.66 us
where the time goes in v5:
time: 49.6 us; the launch traced here: 49.5 us
  Pallas kernels  48.8 us (98%)
  local copies, waits for them, and re-layouts  0.66 us (1%)
    pallas_call x1, Pallas kernels, on_device(): return call(*operands)  48.8 us

profile of v5, /device:TPU:1, one launch (start us, length us, event | category | flops | bytes accessed | tf_op | source)
XLA Modules:
  0.0 49.5 jit_solution(7142191281742335595)
XLA Ops:
  0.0 48.8 %shard_map.145 = f32[8,1,2,2,8,128]{5,4,3,2,1,0:T(8,128)S(1)} custom-call(bf16[1,1,32,32,128]{4,3,2,1,0:T(8,128)(2,1)} %tiles.1, s32[1,1,2,4,128]{4,3,2,1,0:T(4,128)} %targets.1, s32[16]{0:T(128)} %offsets.1, f32[1,128]{1,0:T(1,128)} %bitcast.9, f32[1,128]{1,0:T(1,128)} %bitcast.10, bf16[128,128]{1,0:T(8,128)(2,1)} %wq.1, bf16[128,128]{1,0:T(8,128)(2,1)} %wk.1, ...), custom_call_target="tpu_custom_call" | custom-call | tf_op jit(solution)/shard_map/pallas_call | solution.py:675
  48.8 0.7 %copy.17 = f32[8,1,2,2,8,128]{5,4,3,2,1,0:T(8,128)} copy(f32[8,1,2,2,8,128]{5,4,3,2,1,0:T(8,128)S(1)} %shard_map.145) | data formatting | bytes 262144

commit v6 on v5

--- a/solution.py
+++ b/solution.py
@@ -67,7 +67,7 @@
     at=pltpu.VMEM((R, H, L, L), F32),
     bias_t=pltpu.VMEM((H, L, L), F32),
     lgt=pltpu.VMEM((R, NB, L), F32),
-    lgn=pltpu.VMEM((R * L, C), F32),
+    lgn=pltpu.VMEM((R * L + L, C), F32),
     mirror=pltpu.VMEM((R, NB, L), F32),
     dp=pltpu.VMEM((R, C, L), F32),
     dgt=pltpu.VMEM((R, C, L), BF16),
@@ -606,9 +606,6 @@
 
     lax.fori_loop(0, T - 1, sent, 0)
 
-    pltpu.make_async_copy(m.f_recv, m.f_recv, m.f_sem).wait()
-    out[...] = dot(m.spread[...], m.f_recv[...].reshape(S * 64, C)).reshape(out.shape)
-
     def sent_state(step, carry):
         for pair in range(4):
 
@@ -621,6 +618,9 @@
         return carry
 
     lax.fori_loop(0, S, sent_state, 0)
+
+    pltpu.make_async_copy(m.f_recv, m.f_recv, m.f_sem).wait()
+    out[...] = dot(m.spread[...], m.f_recv[...].reshape(S * 64, C)).reshape(out.shape)
 
 
 def on_device(

time: 49.6 us -> 49.4 us (level)
  no operation moved by 1% of the time
where the time goes in v6:
time: 49.4 us; the launch traced here: 49.3 us
  Pallas kernels  48.6 us (98%)
  local copies, waits for them, and re-layouts  0.66 us (1%)
    pallas_call x1, Pallas kernels, on_device(): return call(*operands)  48.6 us

profile of v6, /device:TPU:1, one launch (start us, length us, event | category | flops | bytes accessed | tf_op | source)
XLA Modules:
  0.0 49.3 jit_solution(1739386163872472472)
XLA Ops:
  0.0 48.6 %shard_map.145 = f32[8,1,2,2,8,128]{5,4,3,2,1,0:T(8,128)S(1)} custom-call(bf16[1,1,32,32,128]{4,3,2,1,0:T(8,128)(2,1)} %tiles.1, s32[1,1,2,4,128]{4,3,2,1,0:T(4,128)} %targets.1, s32[16]{0:T(128)} %offsets.1, f32[1,128]{1,0:T(1,128)} %bitcast.9, f32[1,128]{1,0:T(1,128)} %bitcast.10, bf16[128,128]{1,0:T(8,128)(2,1)} %wq.1, bf16[128,128]{1,0:T(8,128)(2,1)} %wk.1, ...), custom_call_target="tpu_custom_call" | custom-call | tf_op jit(solution)/shard_map/pallas_call | solution.py:675
  48.7 0.7 %copy.17 = f32[8,1,2,2,8,128]{5,4,3,2,1,0:T(8,128)} copy(f32[8,1,2,2,8,128]{5,4,3,2,1,0:T(8,128)S(1)} %shard_map.145) | data formatting | bytes 262144
